TPU v7x, 32 devices: a whole 2x2x4 slice. The times are simulated.
32 devices in a mesh: row: 4 (over y, x), col: 8 (over z, core).
Axes of the slice: x: 2, y: 2, z: 4, core: 2. Of those that a mesh axis runs over, the one named last changes fastest.
Arguments:
- head_start: float32 [1536, 8192], P('row', 'col'), may hold values from -6 to 6
- recharge: float32 [1536, 8192], P('row', 'col'), may hold values from -4 to 4
- storage: float32 [1536, 8192], P('row', 'col'), may hold values from 0.02 to 0.5
- seg_block: int32 [32768], P(('row', 'col')), may hold values from 0 to 3071
- seg_mask: int32 [32768, 128], P(('row', 'col')), may hold values 0 or 1
- seg_cond: float32 [32768, 128], P(('row', 'col')), may hold values from 0.02 to 0.2
- seg_reach: int32 [32768], P(('row', 'col')), may hold values from 0 to 8191, as said below
- reach_bed: float32 [8192], P(('row', 'col')), may hold values from -1 to 1
- section_start: float32 [8192], P(('row', 'col')), may hold values from 0 to 2
- reach_net: int32 [8192], P(('row', 'col')), may hold values from 0 to 63
- net_inflow: float32 [64], replicated, may hold values from 2 to 16
Outputs:
- head: float32 [1536, 8192], P('row', 'col')
- section: float32 [8192], P(('row', 'col'))
Inputs may be any that keep to these rules, and one draw needn't show every extreme that they name: `seg_reach`: A segment on device (i, j) names a reach owned by device (i, j - 1), (i, j) or (i, j + 1), columns taken modulo 8, where reach r is owned by device r // 256 in the numbering i * 8 + j.
All inputs are finite; a program needn't handle non-finite values. No bound on the sum of `seg_mask` on one device may be relied on, other than what follows from the above.
Results may differ from a plain program's by a relative error of at most 0.00029.
Values sent between devices are 32-bit elements; how exact they have to be, the bound alone decides.
A program may use at most 64 MiB of HBM per device.

v0:
```python
import jax
import jax.numpy as jnp
from jax import lax
from jax.sharding import PartitionSpec as P

NETS = 64
PICARD = 2
SWEEPS = 4


def with_halo(cells, sides, width, closed):
    for axis, dim in sides:
        count = lax.axis_size(axis)
        ends = count if closed else count - 1
        head = lax.slice_in_dim(cells, 0, width, axis=dim)
        tail = lax.slice_in_dim(cells, cells.shape[dim] - width, cells.shape[dim], axis=dim)
        cells = jnp.concatenate(
            [
                lax.ppermute(tail, axis, [(i, (i + 1) % count) for i in range(ends)]),
                cells,
                lax.ppermute(head, axis, [((i + 1) % count, i) for i in range(ends)]),
            ],
            axis=dim,
        )
    return cells


def passed_along(array, axis, by):
    length = lax.axis_size(axis)
    return lax.ppermute(array, axis, [(i, (i + by) % length) for i in range(length)])


def relax(padded, storage, supply, cond, source):
    beside = padded[:-2, 1:-1] + padded[2:, 1:-1] + padded[1:-1, :-2] + padded[1:-1, 2:]
    return (beside + supply + source) / (4.0 + storage + cond)


def new_section(bed, inflow, total):
    return bed + jnp.sqrt(1.0 + jax.nn.softplus(inflow - total)) - 1.0


def body(
    head_start,
    recharge,
    storage,
    seg_block,
    seg_mask,
    seg_cond,
    seg_reach,
    reach_bed,
    section_start,
    reach_net,
    net_inflow,
):
    rows, cols = head_start.shape
    blocks = rows * cols // 128
    reaches = reach_bed.shape[0]
    n_col = lax.axis_size("col")
    col_index = lax.axis_index("col")
    weight = seg_mask.astype(jnp.float32) * seg_cond
    cond = jax.ops.segment_sum(weight, seg_block, blocks).reshape(rows, cols)
    picks = (reach_net[:, None] == jnp.arange(NETS, dtype=jnp.int32)[None, :]).astype(jnp.float32)
    inflow = jnp.dot(picks, net_inflow, precision=lax.Precision.HIGHEST)
    supply = storage * head_start + recharge
    owner_col = seg_reach // reaches % n_col
    window_slot = (owner_col - col_index + 1 + n_col) % n_col * reaches + seg_reach % reaches

    def spread(section_own):
        window = with_halo(section_own, (("col", 0),), reaches, True)
        return jnp.take(window, window_slot)

    first_seg = spread(section_start)
    head = head_start
    section_seg = first_seg
    section = section_start
    for step in range(PICARD):
        head_seg = jnp.take(head.reshape(blocks, 128), seg_block, axis=0)
        leak = jnp.sum(weight * (section_seg[:, None] - head_seg), axis=1)
        partial_value = jax.ops.segment_sum(leak, window_slot, 3 * reaches).reshape(3, reaches)
        left_part = passed_along(partial_value[2], "col", 1)
        right_part = passed_along(partial_value[0], "col", -1)
        update_section_own = new_section(
            reach_bed, inflow, partial_value[1] + left_part + right_part
        )
        section = update_section_own
        section_seg = spread(update_section_own)
        source = jax.ops.segment_sum(weight * section_seg[:, None], seg_block, blocks).reshape(
            rows, cols
        )
        for sweep in range(SWEEPS):
            padded = with_halo(head, (("row", 0), ("col", 1)), 1, False)
            head = relax(padded, storage, supply, cond, source)
    return (head, section)


def solution(mesh):
    placed = (
        P("row", "col"),
        P("row", "col"),
        P("row", "col"),
        P(("row", "col")),
        P(("row", "col"), None),
        P(("row", "col"), None),
        P(("row", "col")),
        P(("row", "col")),
        P(("row", "col")),
        P(("row", "col")),
        P(),
    )
    return jax.shard_map(
        body,
        mesh=mesh,
        in_specs=placed,
        out_specs=(P("row", "col"), P(("row", "col"))),
        check_vma=False,
    )
```

profile of v0, /device:TPU:0, one launch (start us, length us, event | category | flops | bytes accessed | tf_op | source)
XLA Modules:
  0.0 259.0 jit_solution(8127691828408697866)
XLA Ops:
  1.1 4.1 %collective-permute-start.5 = (f32[256]{0:T(256)}, f32[256]{0:T(256)S(1)}, u32[]{:S(2)}, u32[]{:S(2)}) collective-permute-start(f32[256]{0:T(256)} %param.23), channel_id=1, source_target_pairs={{1,0},{2,1},{3,2},{4,3},{5,4},{6,5},{7,6},{0,7},{9,8},{10,9},{11,1... | collective-permute-start | bytes 3080 | tf_op jit(solution)/shard_map/ppermute | solution.py:21
  7.4 1.5 reshape.47
  8.9 2.8 %gather_fusion.1 = f32[1024,128]{1,0:T(8,128)S(1)} fusion(f32[3072,128]{1,0:T(8,128)S(1)} %reshape.47, s32[1024]{0:T(1024)S(1)} %fusion.71), kind=kCustom, calls=%fused_computation.1.clone | custom fusion | bytes 1052672 | tf_op jit(solution)/shard_map/jit(_take)/gather | solution.py:77
  11.8 4.5 %gather_fusion = f32[1024]{0:T(1024)S(1)} fusion(f32[768]{0:T(1024)S(1)} %pad_maximum_fusion.88, s32[1024]{0:T(1024)S(1)} %get-tuple-element.11), kind=kCustom, calls=%fused_computation.clone | custom fusion | bytes 12288 | tf_op jit(solution)/shard_map/jit(_take)/gather | solution.py:70
  16.4 1.9 fusion.57
  18.3 7.6 %scatter_custom_fusion = f32[768]{0:T(1024)S(1)} fusion(s32[1024]{0:T(1024)S(1)} %get-tuple-element.12, f32[1024]{0:T(1024)S(1)} %get-tuple-element.7, f32[]{:T(128)} %constant.73.clone.1), kind=kCustom, calls=%fused_computation.203 | custom fusion | flops 1024 | bytes 3076 | tf_op jit(solution)/shard_map/scatter-add | solution.py:79
  26.0 3.5 %collective-permute-start.7 = (f32[256]{0:T(256)S(1)}, f32[256]{0:T(256)S(1)}, u32[]{:S(2)}, u32[]{:S(2)}) collective-permute-start(f32[256]{0:T(256)S(1)} %get-tuple-element.48), channel_id=1, source_target_pairs={{0,7},{1,0},{2,1},{3,2},{4,3},{5,4},{6,5},{7,6},{8,15},{9,8},{10,9... | collective-permute-start | bytes 3080 | tf_op jit(solution)/shard_map/ppermute | solution.py:30
  30.8 3.5 %collective-permute-start.9 = (f32[256]{0:T(256)S(1)}, f32[256]{0:T(256)S(1)}, u32[]{:S(2)}, u32[]{:S(2)}) collective-permute-start(f32[256]{0:T(256)S(1)} %fusion.84), channel_id=1, source_target_pairs={{1,0},{2,1},{3,2},{4,3},{5,4},{6,5},{7,6},{0,7},{9,8},{10,9},{11,1... | collective-permute-start | bytes 3080 | tf_op jit(solution)/shard_map/ppermute | solution.py:21
  34.4 3.8 %collective-permute-start = (f32[1,1024]{1,0:T(1,128)S(1)}, f32[1,1024]{1,0:T(1,128)S(1)}, u32[]{:S(2)}, u32[]{:S(2)}) collective-permute-start(f32[1,1024]{1,0:T(1,128)S(1)} %get-tuple-element.43), channel_id=1, source_target_pairs={{0,8},{8,16},{16,24},{1,9},{9,17},{17,25},{2,10},{10,18},{18,26},{... | collective-permute-start | bytes 12296 | tf_op jit(solution)/shard_map/ppermute | solution.py:19
  38.2 1.3 collective-permute-start.1
  39.5 7.3 %scatter_custom_fusion.2 = f32[3072,128]{1,0:T(8,128)} fusion(s32[1024]{0:T(1024)} %param.18, f32[1024,128]{1,0:T(8,128)S(1)} %get-tuple-element.8, f32[]{:T(128)} %constant.73.clone.1), kind=kCustom, calls=%fused_computation.126 | custom fusion | flops 131072 | bytes 1573376 | tf_op jit(solution)/shard_map/scatter-add | solution.py:61
  46.9 2.6 reshape.49
  49.5 4.5 %gather_fusion.2 = f32[1024]{0:T(1024)S(1)} fusion(f32[768]{0:T(1024)S(1)} %pad_maximum_fusion.89, s32[1024]{0:T(1024)S(1)} %get-tuple-element.11), kind=kCustom, calls=%fused_computation.2.clone | custom fusion | bytes 12288 | tf_op jit(solution)/shard_map/jit(_take)/gather | solution.py:70
  55.9 1.3 collective-permute-start.3
  57.3 7.1 %scatter_custom_fusion.1 = f32[3072,128]{1,0:T(8,128)S(1)} fusion(s32[1024]{0:T(1024)} %param.18, f32[]{:T(128)} %constant.73.clone.1, f32[1024,128]{1,0:T(8,128)S(1)} %get-tuple-element.8, f32[1024]{0:T(1024)S(1)} %broadcast_select_fusion.1), kind=kCustom, calls=%fused_computation.128 | custom fusion | flops 262144 | bytes 2101760 | tf_op jit(solution)/shard_map/scatter-add | solution.py:87
  64.3 1.4 reshape.48
  65.7 7.4 %fusion.45 = (f32[384,1024]{1,0:T(8,128)S(1)}, f32[384,1024]{1,0:T(8,128)S(1)}, f32[384,1024]{1,0:T(8,128)S(1)}) fusion(f32[384,1024]{1,0:T(8,128)} %reshape.48, f32[386,1]{1,0:T(8,128)S(1)} %collective-permute-done.3, f32[1,1024]{1,0:T(1,128)} %copy-done.10, f32[384,1024]{1,0:T(8,128)} %param.15, f32[1,1024]{1,0:T(1,128)} %copy-done.9, ...), kind=kLoop, calls=%fused_computation.112 | loop fusion | flops 7077888 | bytes 12594192 | tf_op jit(solution)/shard_map/div | solution.py:35
  73.2 4.7 %collective-permute-start.10 = (f32[1,1024]{1,0:T(1,128)S(1)}, f32[1,1024]{1,0:T(1,128)S(1)}, u32[]{:S(2)}, u32[]{:S(2)}) collective-permute-start(f32[1,1024]{1,0:T(1,128)S(1)} %get-tuple-element.41), channel_id=1, source_target_pairs={{0,8},{8,16},{16,24},{1,9},{9,17},{17,25},{2,10},{10,18},{18,26},{... | collective-permute-start | bytes 12296 | tf_op jit(solution)/shard_map/ppermute | solution.py:19
  77.9 1.3 collective-permute-start.11
  79.2 4.6 %collective-permute-done.11 = f32[1,1024]{1,0:T(1,128)S(1)} collective-permute-done((f32[1,1024]{1,0:T(1,128)S(1)}, f32[1,1024]{1,0:T(1,128)S(1)}, u32[]{:S(2)}, u32[]{:S(2)}) %collective-permute-start.11) | collective-permute-done | bytes 4128 | tf_op jit(solution)/shard_map/ppermute | solution.py:21
  83.9 2.0 collective-permute-start.12
  87.3 2.0 collective-permute-done.13
  89.3 2.5 fusion.39
  91.8 4.4 %collective-permute-start.14 = (f32[1,1024]{1,0:T(1,128)S(1)}, f32[1,1024]{1,0:T(1,128)S(1)}, u32[]{:S(2)}, u32[]{:S(2)}) collective-permute-start(f32[1,1024]{1,0:T(1,128)S(1)} %get-tuple-element.39), channel_id=1, source_target_pairs={{0,8},{8,16},{16,24},{1,9},{9,17},{17,25},{2,10},{10,18},{18,26},{... | collective-permute-start | bytes 12296 | tf_op jit(solution)/shard_map/ppermute | solution.py:19
  97.5 4.2 %collective-permute-done.15 = f32[1,1024]{1,0:T(1,128)S(1)} collective-permute-done((f32[1,1024]{1,0:T(1,128)S(1)}, f32[1,1024]{1,0:T(1,128)S(1)}, u32[]{:S(2)}, u32[]{:S(2)}) %collective-permute-start.15) | collective-permute-done | bytes 4128 | tf_op jit(solution)/shard_map/ppermute | solution.py:21
  101.9 4.2 %collective-permute-start.16 = (f32[386,1]{1,0:T(8,128)S(1)}, f32[386,1]{1,0:T(8,128)S(1)}, u32[]{:S(2)}, u32[]{:S(2)}) collective-permute-start(f32[386,1]{1,0:T(8,128)S(1)} %get-tuple-element.23), channel_id=1, source_target_pairs={{0,1},{1,2},{2,3},{3,4},{4,5},{5,6},{6,7},{8,9},{9,10},{10,11},{11... | collective-permute-start | bytes 4640 | tf_op jit(solution)/shard_map/ppermute | solution.py:19
  107.4 2.8 %collective-permute-done.17 = f32[386,1]{1,0:T(8,128)S(1)} collective-permute-done((f32[386,1]{1,0:T(8,128)S(1)}, f32[386,1]{1,0:T(8,128)S(1)}, u32[]{:S(2)}, u32[]{:S(2)}) %collective-permute-start.17) | collective-permute-done | bytes 1576 | tf_op jit(solution)/shard_map/ppermute | solution.py:21
  110.2 2.5 fusion.33
  112.7 3.0 %collective-permute-start.18 = (f32[1,1024]{1,0:T(1,128)S(1)}, f32[1,1024]{1,0:T(1,128)S(1)}, u32[]{:S(2)}, u32[]{:S(2)}) collective-permute-start(f32[1,1024]{1,0:T(1,128)S(1)} %get-tuple-element.37), channel_id=1, source_target_pairs={{0,8},{8,16},{16,24},{1,9},{9,17},{17,25},{2,10},{10,18},{18,26},{... | collective-permute-start | bytes 12296 | tf_op jit(solution)/shard_map/ppermute | solution.py:19
  115.7 1.3 collective-permute-start.19
  117.0 4.2 %collective-permute-done.19 = f32[1,1024]{1,0:T(1,128)S(1)} collective-permute-done((f32[1,1024]{1,0:T(1,128)S(1)}, f32[1,1024]{1,0:T(1,128)S(1)}, u32[]{:S(2)}, u32[]{:S(2)}) %collective-permute-start.19) | collective-permute-done | bytes 4128 | tf_op jit(solution)/shard_map/ppermute | solution.py:21
  121.3 4.7 %collective-permute-start.20 = (f32[386,1]{1,0:T(8,128)S(1)}, f32[386,1]{1,0:T(8,128)S(1)}, u32[]{:S(2)}, u32[]{:S(2)}) collective-permute-start(f32[386,1]{1,0:T(8,128)S(1)} %get-tuple-element.21), channel_id=1, source_target_pairs={{0,1},{1,2},{2,3},{3,4},{4,5},{5,6},{6,7},{8,9},{9,10},{10,11},{11... | collective-permute-start | bytes 4640 | tf_op jit(solution)/shard_map/ppermute | solution.py:19
  127.3 2.8 %collective-permute-done.21 = f32[386,1]{1,0:T(8,128)S(1)} collective-permute-done((f32[386,1]{1,0:T(8,128)S(1)}, f32[386,1]{1,0:T(8,128)S(1)}, u32[]{:S(2)}, u32[]{:S(2)}) %collective-permute-start.21) | collective-permute-done | bytes 1576 | tf_op jit(solution)/shard_map/ppermute | solution.py:21
  130.1 3.4 %fusion.27 = f32[384,1024]{1,0:T(8,128)} fusion(f32[384,1024]{1,0:T(8,128)S(1)} %get-tuple-element.6, f32[384,1024]{1,0:T(8,128)S(1)} %copy-done.1, f32[384,1024]{1,0:T(8,128)S(1)} %get-tuple-element.5, f32[386,1]{1,0:T(8,128)S(1)} %collective-permute-done.21, f32[1,1024]{1,0:T(1,128)S(1)} %collective-permute-done.19, f32[384,1024]{1,0:T(8,128)S(1)} %fusion.33, ...), kind=kLoop, calls=%fused_computation.70 | loop fusion | flops 5505024 | bytes 7875600 | tf_op jit(solution)/shard_map/div | solution.py:35
  133.5 2.6 reshape.50
  136.1 5.4 %gather_fusion.3 = f32[1024,128]{1,0:T(8,128)} fusion(f32[3072,128]{1,0:T(8,128)} %reshape.50, s32[1024]{0:T(1024)S(1)} %copy-done.8), kind=kCustom, calls=%fused_computation.4.clone | custom fusion | bytes 1052672 | tf_op jit(solution)/shard_map/jit(_take)/gather | solution.py:77
  141.5 1.7 fusion.55
  143.3 7.8 %scatter_custom_fusion.3 = f32[768]{0:T(1024)S(1)} fusion(s32[1024]{0:T(1024)} %copy-done.14, f32[1024]{0:T(1024)S(1)} %fusion.55, f32[]{:T(128)} %constant.73.clone.1), kind=kCustom, calls=%fused_computation.201 | custom fusion | flops 1024 | bytes 3584 | tf_op jit(solution)/shard_map/scatter-add | solution.py:79
  151.0 4.9 %collective-permute-start.26 = (f32[256]{0:T(256)S(1)}, f32[256]{0:T(256)S(1)}, u32[]{:S(2)}, u32[]{:S(2)}) collective-permute-start(f32[256]{0:T(256)S(1)} %get-tuple-element.45), channel_id=1, source_target_pairs={{0,1},{1,2},{2,3},{3,4},{4,5},{5,6},{6,7},{7,0},{8,9},{9,10},{10,1... | collective-permute-start | bytes 3080 | tf_op jit(solution)/shard_map/ppermute | solution.py:30
  157.7 3.5 %collective-permute-start.29 = (f32[256]{0:T(256)S(1)}, f32[256]{0:T(256)S(1)}, u32[]{:S(2)}, u32[]{:S(2)}) collective-permute-start(f32[256]{0:T(256)S(1)} %fusion.83), channel_id=1, source_target_pairs={{1,0},{2,1},{3,2},{4,3},{5,4},{6,5},{7,6},{0,7},{9,8},{10,9},{11,1... | collective-permute-start | bytes 3080 | tf_op jit(solution)/shard_map/ppermute | solution.py:21
  162.0 2.8 %collective-permute-start.22 = (f32[1,1024]{1,0:T(1,128)S(1)}, f32[1,1024]{1,0:T(1,128)S(1)}, u32[]{:S(2)}, u32[]{:S(2)}) collective-permute-start(f32[1,1024]{1,0:T(1,128)S(1)} %get-tuple-element.35), channel_id=1, source_target_pairs={{0,8},{8,16},{16,24},{1,9},{9,17},{17,25},{2,10},{10,18},{18,26},{... | collective-permute-start | bytes 12296 | tf_op jit(solution)/shard_map/ppermute | solution.py:19
  166.1 8.9 %gather_fusion.4 = f32[1024]{0:T(1024)} fusion(f32[768]{0:T(1024)S(1)} %pad_maximum_fusion.90, s32[1024]{0:T(1024)S(1)} %get-tuple-element.11), kind=kCustom, calls=%fused_computation.3.clone | custom fusion | bytes 12288 | tf_op jit(solution)/shard_map/jit(_take)/gather | solution.py:70
  175.0 1.9 pad_maximum_fusion.75
  176.9 2.5 collective-permute-start.24
  180.7 8.1 %scatter_custom_fusion.4 = f32[3072,128]{1,0:T(8,128)} fusion(s32[1024]{0:T(1024)} %param.18, f32[]{:T(128)} %constant.73.clone.1, f32[1024,128]{1,0:T(8,128)} %copy-done.4, f32[1024]{0:T(1024)S(1)} %broadcast_select_fusion), kind=kCustom, calls=%fused_computation.124 | custom fusion | flops 262144 | bytes 2101760 | tf_op jit(solution)/shard_map/scatter-add | solution.py:87
  188.9 2.6 reshape.51
  191.5 4.8 %fusion.21 = f32[384,1024]{1,0:T(8,128)S(1)} fusion(f32[384,1024]{1,0:T(8,128)S(1)} %get-tuple-element.6, f32[384,1024]{1,0:T(8,128)} %reshape.51, f32[384,1024]{1,0:T(8,128)S(1)} %get-tuple-element.5, f32[386,1]{1,0:T(8,128)} %collective-permute-done.25, f32[1,1024]{1,0:T(1,128)} %copy-done.13, f32[384,1024]{1,0:T(8,128)} %fusion.27, ...), kind=kLoop, calls=%fused_computation.56 | loop fusion | flops 5505024 | bytes 7875600 | tf_op jit(solution)/shard_map/div | solution.py:35
  196.3 4.4 %collective-permute-start.30 = (f32[1,1024]{1,0:T(1,128)S(1)}, f32[1,1024]{1,0:T(1,128)S(1)}, u32[]{:S(2)}, u32[]{:S(2)}) collective-permute-start(f32[1,1024]{1,0:T(1,128)S(1)} %get-tuple-element.33), channel_id=1, source_target_pairs={{0,8},{8,16},{16,24},{1,9},{9,17},{17,25},{2,10},{10,18},{18,26},{... | collective-permute-start | bytes 12296 | tf_op jit(solution)/shard_map/ppermute | solution.py:19
  202.0 4.2 %collective-permute-done.31 = f32[1,1024]{1,0:T(1,128)S(1)} collective-permute-done((f32[1,1024]{1,0:T(1,128)S(1)}, f32[1,1024]{1,0:T(1,128)S(1)}, u32[]{:S(2)}, u32[]{:S(2)}) %collective-permute-start.31) | collective-permute-done | bytes 4128 | tf_op jit(solution)/shard_map/ppermute | solution.py:21
  206.3 2.7 %collective-permute-start.32 = (f32[386,1]{1,0:T(8,128)S(1)}, f32[386,1]{1,0:T(8,128)S(1)}, u32[]{:S(2)}, u32[]{:S(2)}) collective-permute-start(f32[386,1]{1,0:T(8,128)S(1)} %get-tuple-element.17), channel_id=1, source_target_pairs={{0,1},{1,2},{2,3},{3,4},{4,5},{5,6},{6,7},{8,9},{9,10},{10,11},{11... | collective-permute-start | bytes 4640 | tf_op jit(solution)/shard_map/ppermute | solution.py:19
  209.0 1.3 collective-permute-start.33
  210.3 4.7 %collective-permute-done.33 = f32[386,1]{1,0:T(8,128)S(1)} collective-permute-done((f32[386,1]{1,0:T(8,128)S(1)}, f32[386,1]{1,0:T(8,128)S(1)}, u32[]{:S(2)}, u32[]{:S(2)}) %collective-permute-start.33) | collective-permute-done | bytes 1576 | tf_op jit(solution)/shard_map/ppermute | solution.py:21
  215.0 2.5 fusion.15
  217.5 3.7 %collective-permute-start.34 = (f32[1,1024]{1,0:T(1,128)S(1)}, f32[1,1024]{1,0:T(1,128)S(1)}, u32[]{:S(2)}, u32[]{:S(2)}) collective-permute-start(f32[1,1024]{1,0:T(1,128)S(1)} %get-tuple-element.31), channel_id=1, source_target_pairs={{0,8},{8,16},{16,24},{1,9},{9,17},{17,25},{2,10},{10,18},{18,26},{... | collective-permute-start | bytes 12296 | tf_op jit(solution)/shard_map/ppermute | solution.py:19
  222.6 4.2 %collective-permute-done.35 = f32[1,1024]{1,0:T(1,128)S(1)} collective-permute-done((f32[1,1024]{1,0:T(1,128)S(1)}, f32[1,1024]{1,0:T(1,128)S(1)}, u32[]{:S(2)}, u32[]{:S(2)}) %collective-permute-start.35) | collective-permute-done | bytes 4128 | tf_op jit(solution)/shard_map/ppermute | solution.py:21
  226.9 4.9 %collective-permute-start.36 = (f32[386,1]{1,0:T(8,128)S(1)}, f32[386,1]{1,0:T(8,128)S(1)}, u32[]{:S(2)}, u32[]{:S(2)}) collective-permute-start(f32[386,1]{1,0:T(8,128)S(1)} %get-tuple-element.15), channel_id=1, source_target_pairs={{0,1},{1,2},{2,3},{3,4},{4,5},{5,6},{6,7},{8,9},{9,10},{10,11},{11... | collective-permute-start | bytes 4640 | tf_op jit(solution)/shard_map/ppermute | solution.py:19
  233.1 2.8 %collective-permute-done.37 = f32[386,1]{1,0:T(8,128)S(1)} collective-permute-done((f32[386,1]{1,0:T(8,128)S(1)}, f32[386,1]{1,0:T(8,128)S(1)}, u32[]{:S(2)}, u32[]{:S(2)}) %collective-permute-start.37) | collective-permute-done | bytes 1576 | tf_op jit(solution)/shard_map/ppermute | solution.py:21
  235.9 2.5 fusion.9
  238.4 2.8 %collective-permute-start.38 = (f32[1,1024]{1,0:T(1,128)S(1)}, f32[1,1024]{1,0:T(1,128)S(1)}, u32[]{:S(2)}, u32[]{:S(2)}) collective-permute-start(f32[1,1024]{1,0:T(1,128)S(1)} %get-tuple-element.29), channel_id=1, source_target_pairs={{0,8},{8,16},{16,24},{1,9},{9,17},{17,25},{2,10},{10,18},{18,26},{... | collective-permute-start | bytes 12296 | tf_op jit(solution)/shard_map/ppermute | solution.py:19
  241.2 1.3 collective-permute-start.39
  242.6 4.2 %collective-permute-done.39 = f32[1,1024]{1,0:T(1,128)S(1)} collective-permute-done((f32[1,1024]{1,0:T(1,128)S(1)}, f32[1,1024]{1,0:T(1,128)S(1)}, u32[]{:S(2)}, u32[]{:S(2)}) %collective-permute-start.39) | collective-permute-done | bytes 4128 | tf_op jit(solution)/shard_map/ppermute | solution.py:21
  246.9 4.7 %collective-permute-start.40 = (f32[386,1]{1,0:T(8,128)S(1)}, f32[386,1]{1,0:T(8,128)S(1)}, u32[]{:S(2)}, u32[]{:S(2)}) collective-permute-start(f32[386,1]{1,0:T(8,128)S(1)} %get-tuple-element.13), channel_id=1, source_target_pairs={{0,1},{1,2},{2,3},{3,4},{4,5},{5,6},{6,7},{8,9},{9,10},{10,11},{11... | collective-permute-start | bytes 4640 | tf_op jit(solution)/shard_map/ppermute | solution.py:19
  252.9 2.8 %collective-permute-done.41 = f32[386,1]{1,0:T(8,128)S(1)} collective-permute-done((f32[386,1]{1,0:T(8,128)S(1)}, f32[386,1]{1,0:T(8,128)S(1)}, u32[]{:S(2)}, u32[]{:S(2)}) %collective-permute-start.41) | collective-permute-done | bytes 1576 | tf_op jit(solution)/shard_map/ppermute | solution.py:21
  255.7 3.4 %fusion.3 = f32[384,1024]{1,0:T(8,128)} fusion(f32[384,1024]{1,0:T(8,128)S(1)} %get-tuple-element.6, f32[384,1024]{1,0:T(8,128)S(1)} %copy-done.2, f32[384,1024]{1,0:T(8,128)S(1)} %get-tuple-element.5, f32[386,1]{1,0:T(8,128)S(1)} %collective-permute-done.41, f32[1,1024]{1,0:T(1,128)S(1)} %collective-permute-done.39, f32[384,1024]{1,0:T(8,128)S(1)} %fusion.9, ...), kind=kLoop, calls=%fused_computation.14 | loop fusion | flops 5505024 | bytes 7875600 | tf_op jit(solution)/shard_map/div | solution.py:35
  (129 shorter events, 22.3 us)
Async XLA Ops:
  0.6 28.9 %copy-start = (f32[64]{0:T(128)S(1)}, f32[64]{0:T(128)}, u32[]{:S(2)}) copy-start(f32[64]{0:T(128)} %param.25) | copy-start | bytes 772
  0.6 11.1 %collective-permute-start.4 = (f32[256]{0:T(256)}, f32[256]{0:T(256)S(1)}, u32[]{:S(2)}, u32[]{:S(2)}) collective-permute-start(f32[256]{0:T(256)} %param.23), channel_id=1, source_target_pairs={{0,1},{1,2},{2,3},{3,4},{4,5},{5,6},{6,7},{7,0},{8,9},{9,10},{10,1... | collective-permute-start | bytes 3080 | tf_op jit(solution)/shard_map/ppermute | solution.py:19
  1.1 10.6 %collective-permute-start.5 = (f32[256]{0:T(256)}, f32[256]{0:T(256)S(1)}, u32[]{:S(2)}, u32[]{:S(2)}) collective-permute-start(f32[256]{0:T(256)} %param.23), channel_id=1, source_target_pairs={{1,0},{2,1},{3,2},{4,3},{5,4},{6,5},{7,6},{0,7},{9,8},{10,9},{11,1... | collective-permute-start | bytes 3080 | tf_op jit(solution)/shard_map/ppermute | solution.py:21
  5.9 3.0 %copy-start.7 = (s32[1024]{0:T(1024)}, s32[1024]{0:T(1024)S(1)}, u32[]{:S(2)}) copy-start(s32[1024]{0:T(1024)S(1)} %fusion.71) | copy-start | bytes 12292
  6.7 11.6 %copy-start.14 = (s32[1024]{0:T(1024)}, s32[1024]{0:T(1024)S(1)}, u32[]{:S(2)}) copy-start(s32[1024]{0:T(1024)S(1)} %get-tuple-element.12) | copy-start | bytes 12292
  7.4 9.0 %copy-start.16 = (pred[1024]{0:T(1024)(128)(4,1)}, pred[1024]{0:T(1024)(128)(4,1)S(1)}, u32[]{:S(2)}) copy-start(pred[1024]{0:T(1024)(128)(4,1)S(1)} %compare_and_fusion.1) | copy-start | bytes 3076
  8.9 2.9 %copy-start.25 = (f32[256]{0:T(256)S(1)}, f32[256]{0:T(256)}, u32[]{:S(2)}) copy-start(f32[256]{0:T(256)} %param.23) | copy-start | bytes 3076
  16.3 13.2 %copy-start.26 = (s32[256]{0:T(256)S(1)}, s32[256]{0:T(256)}, u32[]{:S(2)}) copy-start(s32[256]{0:T(256)} %param.24) | copy-start | bytes 3076
  16.3 14.5 %copy-start.21 = (f32[256]{0:T(256)S(1)}, f32[256]{0:T(256)}, u32[]{:S(2)}) copy-start(f32[256]{0:T(256)} %param.22) | copy-start | bytes 3076
  16.3 18.0 %copy-start.3 = (f32[384,1024]{1,0:T(8,128)S(1)}, f32[384,1024]{1,0:T(8,128)}, u32[]{:S(2)}) copy-start(f32[384,1024]{1,0:T(8,128)} %param.15) | copy-start | bytes 4718596
  16.4 40.9 %copy-start.18 = (pred[1024]{0:T(1024)(128)(4,1)}, pred[1024]{0:T(1024)(128)(4,1)S(1)}, u32[]{:S(2)}) copy-start(pred[1024]{0:T(1024)(128)(4,1)S(1)} %get-tuple-element.10) | copy-start | bytes 3076
  18.3 39.0 %copy-start.4 = (f32[1024,128]{1,0:T(8,128)}, f32[1024,128]{1,0:T(8,128)S(1)}, u32[]{:S(2)}) copy-start(f32[1024,128]{1,0:T(8,128)S(1)} %get-tuple-element.8) | copy-start | bytes 1572868
  25.9 4.8 %collective-permute-start.6 = (f32[256]{0:T(256)S(1)}, f32[256]{0:T(256)S(1)}, u32[]{:S(2)}, u32[]{:S(2)}) collective-permute-start(f32[256]{0:T(256)S(1)} %get-tuple-element.47), channel_id=1, source_target_pairs={{0,1},{1,2},{2,3},{3,4},{4,5},{5,6},{6,7},{7,0},{8,9},{9,10},{10,1... | collective-permute-start | bytes 3080 | tf_op jit(solution)/shard_map/ppermute | solution.py:30
  26.0 4.8 %collective-permute-start.7 = (f32[256]{0:T(256)S(1)}, f32[256]{0:T(256)S(1)}, u32[]{:S(2)}, u32[]{:S(2)}) collective-permute-start(f32[256]{0:T(256)S(1)} %get-tuple-element.48), channel_id=1, source_target_pairs={{0,7},{1,0},{2,1},{3,2},{4,3},{5,4},{6,5},{7,6},{8,15},{9,8},{10,9... | collective-permute-start | bytes 3080 | tf_op jit(solution)/shard_map/ppermute | solution.py:30
  29.7 19.8 %copy-start.23 = (f32[1,256]{1,0:T(1,128)}, f32[1,256]{1,0:T(1,128)S(1)}, u32[]{:S(2)}) copy-start(f32[1,256]{1,0:T(1,128)S(1)} %fusion.62) | copy-start | bytes 3076
  30.8 18.6 %collective-permute-start.9 = (f32[256]{0:T(256)S(1)}, f32[256]{0:T(256)S(1)}, u32[]{:S(2)}, u32[]{:S(2)}) collective-permute-start(f32[256]{0:T(256)S(1)} %fusion.84), channel_id=1, source_target_pairs={{1,0},{2,1},{3,2},{4,3},{5,4},{6,5},{7,6},{0,7},{9,8},{10,9},{11,1... | collective-permute-start | bytes 3080 | tf_op jit(solution)/shard_map/ppermute | solution.py:21
  34.4 15.1 %collective-permute-start.8 = (f32[256]{0:T(256)S(1)}, f32[256]{0:T(256)S(1)}, u32[]{:S(2)}, u32[]{:S(2)}) collective-permute-start(f32[256]{0:T(256)S(1)} %fusion.84), channel_id=1, source_target_pairs={{0,1},{1,2},{2,3},{3,4},{4,5},{5,6},{6,7},{7,0},{8,9},{9,10},{10,1... | collective-permute-start | bytes 3080 | tf_op jit(solution)/shard_map/ppermute | solution.py:19
  34.4 19.6 %collective-permute-start = (f32[1,1024]{1,0:T(1,128)S(1)}, f32[1,1024]{1,0:T(1,128)S(1)}, u32[]{:S(2)}, u32[]{:S(2)}) collective-permute-start(f32[1,1024]{1,0:T(1,128)S(1)} %get-tuple-element.43), channel_id=1, source_target_pairs={{0,8},{8,16},{16,24},{1,9},{9,17},{17,25},{2,10},{10,18},{18,26},{... | collective-permute-start | bytes 12296 | tf_op jit(solution)/shard_map/ppermute | solution.py:19
  38.2 15.8 %collective-permute-start.1 = (f32[1,1024]{1,0:T(1,128)S(1)}, f32[1,1024]{1,0:T(1,128)S(1)}, u32[]{:S(2)}, u32[]{:S(2)}) collective-permute-start(f32[1,1024]{1,0:T(1,128)S(1)} %get-tuple-element.44), channel_id=1, source_target_pairs={{8,0},{16,8},{24,16},{9,1},{17,9},{25,17},{10,2},{18,10},{26,18},{... | collective-permute-start | bytes 12296 | tf_op jit(solution)/shard_map/ppermute | solution.py:21
  54.6 11.1 %collective-permute-start.2 = (f32[386,1]{1,0:T(8,128)S(1)}, f32[386,1]{1,0:T(8,128)S(1)}, u32[]{:S(2)}, u32[]{:S(2)}) collective-permute-start(f32[386,1]{1,0:T(8,128)S(1)} %get-tuple-element.27), channel_id=1, source_target_pairs={{0,1},{1,2},{2,3},{3,4},{4,5},{5,6},{6,7},{8,9},{9,10},{10,11},{11... | collective-permute-start | bytes 4640 | tf_op jit(solution)/shard_map/ppermute | solution.py:19
  55.9 9.8 %collective-permute-start.3 = (f32[386,1]{1,0:T(8,128)S(1)}, f32[386,1]{1,0:T(8,128)S(1)}, u32[]{:S(2)}, u32[]{:S(2)}) collective-permute-start(f32[386,1]{1,0:T(8,128)S(1)} %get-tuple-element.28), channel_id=1, source_target_pairs={{1,0},{2,1},{3,2},{4,3},{5,4},{6,5},{7,6},{9,8},{10,9},{11,10},{12... | collective-permute-start | bytes 4640 | tf_op jit(solution)/shard_map/ppermute | solution.py:21
  57.3 8.4 %copy-start.5 = (f32[1024]{0:T(1024)}, f32[1024]{0:T(1024)S(1)}, u32[]{:S(2)}) copy-start(f32[1024]{0:T(1024)S(1)} %broadcast_select_fusion.1) | copy-start | bytes 12292
  73.2 16.1 %copy-start.1 = (f32[384,1024]{1,0:T(8,128)S(1)}, f32[384,1024]{1,0:T(8,128)}, u32[]{:S(2)}) copy-start(f32[384,1024]{1,0:T(8,128)} %reshape.48) | copy-start | bytes 4718596
  73.2 6.0 %collective-permute-start.10 = (f32[1,1024]{1,0:T(1,128)S(1)}, f32[1,1024]{1,0:T(1,128)S(1)}, u32[]{:S(2)}, u32[]{:S(2)}) collective-permute-start(f32[1,1024]{1,0:T(1,128)S(1)} %get-tuple-element.41), channel_id=1, source_target_pairs={{0,8},{8,16},{16,24},{1,9},{9,17},{17,25},{2,10},{10,18},{18,26},{... | collective-permute-start | bytes 12296 | tf_op jit(solution)/shard_map/ppermute | solution.py:19
  77.9 5.9 %collective-permute-start.11 = (f32[1,1024]{1,0:T(1,128)S(1)}, f32[1,1024]{1,0:T(1,128)S(1)}, u32[]{:S(2)}, u32[]{:S(2)}) collective-permute-start(f32[1,1024]{1,0:T(1,128)S(1)} %get-tuple-element.42), channel_id=1, source_target_pairs={{8,0},{16,8},{24,16},{9,1},{17,9},{25,17},{10,2},{18,10},{26,18},{... | collective-permute-start | bytes 12296 | tf_op jit(solution)/shard_map/ppermute | solution.py:21
  83.9 3.3 %collective-permute-start.12 = (f32[386,1]{1,0:T(8,128)S(1)}, f32[386,1]{1,0:T(8,128)S(1)}, u32[]{:S(2)}, u32[]{:S(2)}) collective-permute-start(f32[386,1]{1,0:T(8,128)S(1)} %get-tuple-element.25), channel_id=1, source_target_pairs={{0,1},{1,2},{2,3},{3,4},{4,5},{5,6},{6,7},{8,9},{9,10},{10,11},{11... | collective-permute-start | bytes 4640 | tf_op jit(solution)/shard_map/ppermute | solution.py:19
  85.9 3.3 %collective-permute-start.13 = (f32[386,1]{1,0:T(8,128)S(1)}, f32[386,1]{1,0:T(8,128)S(1)}, u32[]{:S(2)}, u32[]{:S(2)}) collective-permute-start(f32[386,1]{1,0:T(8,128)S(1)} %get-tuple-element.26), channel_id=1, source_target_pairs={{1,0},{2,1},{3,2},{4,3},{5,4},{6,5},{7,6},{9,8},{10,9},{11,10},{12... | collective-permute-start | bytes 4640 | tf_op jit(solution)/shard_map/ppermute | solution.py:21
  91.8 5.7 %collective-permute-start.14 = (f32[1,1024]{1,0:T(1,128)S(1)}, f32[1,1024]{1,0:T(1,128)S(1)}, u32[]{:S(2)}, u32[]{:S(2)}) collective-permute-start(f32[1,1024]{1,0:T(1,128)S(1)} %get-tuple-element.39), channel_id=1, source_target_pairs={{0,8},{8,16},{16,24},{1,9},{9,17},{17,25},{2,10},{10,18},{18,26},{... | collective-permute-start | bytes 12296 | tf_op jit(solution)/shard_map/ppermute | solution.py:19
  96.2 5.5 %collective-permute-start.15 = (f32[1,1024]{1,0:T(1,128)S(1)}, f32[1,1024]{1,0:T(1,128)S(1)}, u32[]{:S(2)}, u32[]{:S(2)}) collective-permute-start(f32[1,1024]{1,0:T(1,128)S(1)} %get-tuple-element.40), channel_id=1, source_target_pairs={{8,0},{16,8},{24,16},{9,1},{17,9},{25,17},{10,2},{18,10},{26,18},{... | collective-permute-start | bytes 12296 | tf_op jit(solution)/shard_map/ppermute | solution.py:21
  101.9 5.5 %collective-permute-start.16 = (f32[386,1]{1,0:T(8,128)S(1)}, f32[386,1]{1,0:T(8,128)S(1)}, u32[]{:S(2)}, u32[]{:S(2)}) collective-permute-start(f32[386,1]{1,0:T(8,128)S(1)} %get-tuple-element.23), channel_id=1, source_target_pairs={{0,1},{1,2},{2,3},{3,4},{4,5},{5,6},{6,7},{8,9},{9,10},{10,11},{11... | collective-permute-start | bytes 4640 | tf_op jit(solution)/shard_map/ppermute | solution.py:19
  106.1 4.1 %collective-permute-start.17 = (f32[386,1]{1,0:T(8,128)S(1)}, f32[386,1]{1,0:T(8,128)S(1)}, u32[]{:S(2)}, u32[]{:S(2)}) collective-permute-start(f32[386,1]{1,0:T(8,128)S(1)} %get-tuple-element.24), channel_id=1, source_target_pairs={{1,0},{2,1},{3,2},{4,3},{5,4},{6,5},{7,6},{9,8},{10,9},{11,10},{12... | collective-permute-start | bytes 4640 | tf_op jit(solution)/shard_map/ppermute | solution.py:21
  112.7 4.3 %collective-permute-start.18 = (f32[1,1024]{1,0:T(1,128)S(1)}, f32[1,1024]{1,0:T(1,128)S(1)}, u32[]{:S(2)}, u32[]{:S(2)}) collective-permute-start(f32[1,1024]{1,0:T(1,128)S(1)} %get-tuple-element.37), channel_id=1, source_target_pairs={{0,8},{8,16},{16,24},{1,9},{9,17},{17,25},{2,10},{10,18},{18,26},{... | collective-permute-start | bytes 12296 | tf_op jit(solution)/shard_map/ppermute | solution.py:19
  115.7 5.5 %collective-permute-start.19 = (f32[1,1024]{1,0:T(1,128)S(1)}, f32[1,1024]{1,0:T(1,128)S(1)}, u32[]{:S(2)}, u32[]{:S(2)}) collective-permute-start(f32[1,1024]{1,0:T(1,128)S(1)} %get-tuple-element.38), channel_id=1, source_target_pairs={{8,0},{16,8},{24,16},{9,1},{17,9},{25,17},{10,2},{18,10},{26,18},{... | collective-permute-start | bytes 12296 | tf_op jit(solution)/shard_map/ppermute | solution.py:21
  121.3 6.0 %collective-permute-start.20 = (f32[386,1]{1,0:T(8,128)S(1)}, f32[386,1]{1,0:T(8,128)S(1)}, u32[]{:S(2)}, u32[]{:S(2)}) collective-permute-start(f32[386,1]{1,0:T(8,128)S(1)} %get-tuple-element.21), channel_id=1, source_target_pairs={{0,1},{1,2},{2,3},{3,4},{4,5},{5,6},{6,7},{8,9},{9,10},{10,11},{11... | collective-permute-start | bytes 4640 | tf_op jit(solution)/shard_map/ppermute | solution.py:19
  126.0 4.1 %collective-permute-start.21 = (f32[386,1]{1,0:T(8,128)S(1)}, f32[386,1]{1,0:T(8,128)S(1)}, u32[]{:S(2)}, u32[]{:S(2)}) collective-permute-start(f32[386,1]{1,0:T(8,128)S(1)} %get-tuple-element.22), channel_id=1, source_target_pairs={{1,0},{2,1},{3,2},{4,3},{5,4},{6,5},{7,6},{9,8},{10,9},{11,10},{12... | collective-permute-start | bytes 4640 | tf_op jit(solution)/shard_map/ppermute | solution.py:21
  136.1 5.5 %copy-start.6 = (f32[1024]{0:T(1024)S(1)}, f32[1024]{0:T(1024)}, u32[]{:S(2)}) copy-start(f32[1024]{0:T(1024)} %copy-done.5) | copy-start | bytes 12292
  136.1 5.5 %copy-start.17 = (pred[1024]{0:T(1024)(128)(4,1)S(1)}, pred[1024]{0:T(1024)(128)(4,1)}, u32[]{:S(2)}) copy-start(pred[1024]{0:T(1024)(128)(4,1)} %copy-done.16) | copy-start | bytes 3076
  136.1 21.5 %copy-start.22 = (f32[256]{0:T(256)S(1)}, f32[256]{0:T(256)}, u32[]{:S(2)}) copy-start(f32[256]{0:T(256)} %param.22) | copy-start | bytes 3076
  136.1 21.5 %copy-start.24 = (f32[1,256]{1,0:T(1,128)S(1)}, f32[1,256]{1,0:T(1,128)}, u32[]{:S(2)}) copy-start(f32[1,256]{1,0:T(1,128)} %copy-done.23) | copy-start | bytes 3076
  151.0 6.5 %collective-permute-start.26 = (f32[256]{0:T(256)S(1)}, f32[256]{0:T(256)S(1)}, u32[]{:S(2)}, u32[]{:S(2)}) collective-permute-start(f32[256]{0:T(256)S(1)} %get-tuple-element.45), channel_id=1, source_target_pairs={{0,1},{1,2},{2,3},{3,4},{4,5},{5,6},{6,7},{7,0},{8,9},{9,10},{10,1... | collective-permute-start | bytes 3080 | tf_op jit(solution)/shard_map/ppermute | solution.py:30
  155.9 1.7 collective-permute-start.27
  157.6 17.3 %copy-start.20 = (f32[256]{0:T(256)}, f32[256]{0:T(256)S(1)}, u32[]{:S(2)}) copy-start(f32[256]{0:T(256)S(1)} %fusion.83) | copy-start | bytes 3076
  157.7 8.4 %collective-permute-start.29 = (f32[256]{0:T(256)S(1)}, f32[256]{0:T(256)S(1)}, u32[]{:S(2)}, u32[]{:S(2)}) collective-permute-start(f32[256]{0:T(256)S(1)} %fusion.83), channel_id=1, source_target_pairs={{1,0},{2,1},{3,2},{4,3},{5,4},{6,5},{7,6},{0,7},{9,8},{10,9},{11,1... | collective-permute-start | bytes 3080 | tf_op jit(solution)/shard_map/ppermute | solution.py:21
  161.2 4.9 %collective-permute-start.28 = (f32[256]{0:T(256)S(1)}, f32[256]{0:T(256)S(1)}, u32[]{:S(2)}, u32[]{:S(2)}) collective-permute-start(f32[256]{0:T(256)S(1)} %fusion.83), channel_id=1, source_target_pairs={{0,1},{1,2},{2,3},{3,4},{4,5},{5,6},{6,7},{7,0},{8,9},{9,10},{10,1... | collective-permute-start | bytes 3080 | tf_op jit(solution)/shard_map/ppermute | solution.py:19
  162.0 13.0 %collective-permute-start.22 = (f32[1,1024]{1,0:T(1,128)S(1)}, f32[1,1024]{1,0:T(1,128)S(1)}, u32[]{:S(2)}, u32[]{:S(2)}) collective-permute-start(f32[1,1024]{1,0:T(1,128)S(1)} %get-tuple-element.35), channel_id=1, source_target_pairs={{0,8},{8,16},{16,24},{1,9},{9,17},{17,25},{2,10},{10,18},{18,26},{... | collective-permute-start | bytes 12296 | tf_op jit(solution)/shard_map/ppermute | solution.py:19
  164.8 10.2 %collective-permute-start.23 = (f32[1,1024]{1,0:T(1,128)S(1)}, f32[1,1024]{1,0:T(1,128)S(1)}, u32[]{:S(2)}, u32[]{:S(2)}) collective-permute-start(f32[1,1024]{1,0:T(1,128)S(1)} %get-tuple-element.36), channel_id=1, source_target_pairs={{8,0},{16,8},{24,16},{9,1},{17,9},{25,17},{10,2},{18,10},{26,18},{... | collective-permute-start | bytes 12296 | tf_op jit(solution)/shard_map/ppermute | solution.py:21
  175.0 5.7 %copy-start.15 = (f32[1024]{0:T(1024)S(1)}, f32[1024]{0:T(1024)}, u32[]{:S(2)}) copy-start(f32[1024]{0:T(1024)} %gather_fusion.4) | copy-start | bytes 12292
  175.0 5.7 %copy-start.19 = (pred[1024]{0:T(1024)(128)(4,1)S(1)}, pred[1024]{0:T(1024)(128)(4,1)}, u32[]{:S(2)}) copy-start(pred[1024]{0:T(1024)(128)(4,1)} %copy-done.18) | copy-start | bytes 3076
  176.9 14.6 %collective-permute-start.24 = (f32[386,1]{1,0:T(8,128)}, f32[386,1]{1,0:T(8,128)S(1)}, u32[]{:S(2)}, u32[]{:S(2)}) collective-permute-start(f32[386,1]{1,0:T(8,128)} %get-tuple-element.19), channel_id=1, source_target_pairs={{0,1},{1,2},{2,3},{3,4},{4,5},{5,6},{6,7},{8,9},{9,10},{10,11},{11... | collective-permute-start | bytes 4640 | tf_op jit(solution)/shard_map/ppermute | solution.py:19
  179.4 12.1 %collective-permute-start.25 = (f32[386,1]{1,0:T(8,128)S(1)}, f32[386,1]{1,0:T(8,128)}, u32[]{:S(2)}, u32[]{:S(2)}) collective-permute-start(f32[386,1]{1,0:T(8,128)S(1)} %get-tuple-element.20), channel_id=1, source_target_pairs={{1,0},{2,1},{3,2},{4,3},{5,4},{6,5},{7,6},{9,8},{10,9},{11,10},{12... | collective-permute-start | bytes 4640 | tf_op jit(solution)/shard_map/ppermute | solution.py:21
  188.9 2.6 %copy-start.12 = (f32[1,1024]{1,0:T(1,128)S(1)}, f32[1,1024]{1,0:T(1,128)}, u32[]{:S(2)}) copy-start(f32[1,1024]{1,0:T(1,128)} %copy-done.11) | copy-start | bytes 12292
  196.2 18.8 %copy-start.2 = (f32[384,1024]{1,0:T(8,128)S(1)}, f32[384,1024]{1,0:T(8,128)}, u32[]{:S(2)}) copy-start(f32[384,1024]{1,0:T(8,128)} %reshape.51) | copy-start | bytes 4718596
  196.3 5.7 %collective-permute-start.30 = (f32[1,1024]{1,0:T(1,128)S(1)}, f32[1,1024]{1,0:T(1,128)S(1)}, u32[]{:S(2)}, u32[]{:S(2)}) collective-permute-start(f32[1,1024]{1,0:T(1,128)S(1)} %get-tuple-element.33), channel_id=1, source_target_pairs={{0,8},{8,16},{16,24},{1,9},{9,17},{17,25},{2,10},{10,18},{18,26},{... | collective-permute-start | bytes 12296 | tf_op jit(solution)/shard_map/ppermute | solution.py:19
  200.7 5.5 %collective-permute-start.31 = (f32[1,1024]{1,0:T(1,128)S(1)}, f32[1,1024]{1,0:T(1,128)S(1)}, u32[]{:S(2)}, u32[]{:S(2)}) collective-permute-start(f32[1,1024]{1,0:T(1,128)S(1)} %get-tuple-element.34), channel_id=1, source_target_pairs={{8,0},{16,8},{24,16},{9,1},{17,9},{25,17},{10,2},{18,10},{26,18},{... | collective-permute-start | bytes 12296 | tf_op jit(solution)/shard_map/ppermute | solution.py:21
  206.3 4.0 %collective-permute-start.32 = (f32[386,1]{1,0:T(8,128)S(1)}, f32[386,1]{1,0:T(8,128)S(1)}, u32[]{:S(2)}, u32[]{:S(2)}) collective-permute-start(f32[386,1]{1,0:T(8,128)S(1)} %get-tuple-element.17), channel_id=1, source_target_pairs={{0,1},{1,2},{2,3},{3,4},{4,5},{5,6},{6,7},{8,9},{9,10},{10,11},{11... | collective-permute-start | bytes 4640 | tf_op jit(solution)/shard_map/ppermute | solution.py:19
  209.0 6.0 %collective-permute-start.33 = (f32[386,1]{1,0:T(8,128)S(1)}, f32[386,1]{1,0:T(8,128)S(1)}, u32[]{:S(2)}, u32[]{:S(2)}) collective-permute-start(f32[386,1]{1,0:T(8,128)S(1)} %get-tuple-element.18), channel_id=1, source_target_pairs={{1,0},{2,1},{3,2},{4,3},{5,4},{6,5},{7,6},{9,8},{10,9},{11,10},{12... | collective-permute-start | bytes 4640 | tf_op jit(solution)/shard_map/ppermute | solution.py:21
  217.5 5.0 %collective-permute-start.34 = (f32[1,1024]{1,0:T(1,128)S(1)}, f32[1,1024]{1,0:T(1,128)S(1)}, u32[]{:S(2)}, u32[]{:S(2)}) collective-permute-start(f32[1,1024]{1,0:T(1,128)S(1)} %get-tuple-element.31), channel_id=1, source_target_pairs={{0,8},{8,16},{16,24},{1,9},{9,17},{17,25},{2,10},{10,18},{18,26},{... | collective-permute-start | bytes 12296 | tf_op jit(solution)/shard_map/ppermute | solution.py:19
  221.2 5.5 %collective-permute-start.35 = (f32[1,1024]{1,0:T(1,128)S(1)}, f32[1,1024]{1,0:T(1,128)S(1)}, u32[]{:S(2)}, u32[]{:S(2)}) collective-permute-start(f32[1,1024]{1,0:T(1,128)S(1)} %get-tuple-element.32), channel_id=1, source_target_pairs={{8,0},{16,8},{24,16},{9,1},{17,9},{25,17},{10,2},{18,10},{26,18},{... | collective-permute-start | bytes 12296 | tf_op jit(solution)/shard_map/ppermute | solution.py:21
  226.9 6.2 %collective-permute-start.36 = (f32[386,1]{1,0:T(8,128)S(1)}, f32[386,1]{1,0:T(8,128)S(1)}, u32[]{:S(2)}, u32[]{:S(2)}) collective-permute-start(f32[386,1]{1,0:T(8,128)S(1)} %get-tuple-element.15), channel_id=1, source_target_pairs={{0,1},{1,2},{2,3},{3,4},{4,5},{5,6},{6,7},{8,9},{9,10},{10,11},{11... | collective-permute-start | bytes 4640 | tf_op jit(solution)/shard_map/ppermute | solution.py:19
  231.8 4.1 %collective-permute-start.37 = (f32[386,1]{1,0:T(8,128)S(1)}, f32[386,1]{1,0:T(8,128)S(1)}, u32[]{:S(2)}, u32[]{:S(2)}) collective-permute-start(f32[386,1]{1,0:T(8,128)S(1)} %get-tuple-element.16), channel_id=1, source_target_pairs={{1,0},{2,1},{3,2},{4,3},{5,4},{6,5},{7,6},{9,8},{10,9},{11,10},{12... | collective-permute-start | bytes 4640 | tf_op jit(solution)/shard_map/ppermute | solution.py:21
  238.4 4.1 %collective-permute-start.38 = (f32[1,1024]{1,0:T(1,128)S(1)}, f32[1,1024]{1,0:T(1,128)S(1)}, u32[]{:S(2)}, u32[]{:S(2)}) collective-permute-start(f32[1,1024]{1,0:T(1,128)S(1)} %get-tuple-element.29), channel_id=1, source_target_pairs={{0,8},{8,16},{16,24},{1,9},{9,17},{17,25},{2,10},{10,18},{18,26},{... | collective-permute-start | bytes 12296 | tf_op jit(solution)/shard_map/ppermute | solution.py:19
  241.2 5.5 %collective-permute-start.39 = (f32[1,1024]{1,0:T(1,128)S(1)}, f32[1,1024]{1,0:T(1,128)S(1)}, u32[]{:S(2)}, u32[]{:S(2)}) collective-permute-start(f32[1,1024]{1,0:T(1,128)S(1)} %get-tuple-element.30), channel_id=1, source_target_pairs={{8,0},{16,8},{24,16},{9,1},{17,9},{25,17},{10,2},{18,10},{26,18},{... | collective-permute-start | bytes 12296 | tf_op jit(solution)/shard_map/ppermute | solution.py:21
  246.9 6.0 %collective-permute-start.40 = (f32[386,1]{1,0:T(8,128)S(1)}, f32[386,1]{1,0:T(8,128)S(1)}, u32[]{:S(2)}, u32[]{:S(2)}) collective-permute-start(f32[386,1]{1,0:T(8,128)S(1)} %get-tuple-element.13), channel_id=1, source_target_pairs={{0,1},{1,2},{2,3},{3,4},{4,5},{5,6},{6,7},{8,9},{9,10},{10,11},{11... | collective-permute-start | bytes 4640 | tf_op jit(solution)/shard_map/ppermute | solution.py:19
  251.6 4.1 %collective-permute-start.41 = (f32[386,1]{1,0:T(8,128)S(1)}, f32[386,1]{1,0:T(8,128)S(1)}, u32[]{:S(2)}, u32[]{:S(2)}) collective-permute-start(f32[386,1]{1,0:T(8,128)S(1)} %get-tuple-element.14), channel_id=1, source_target_pairs={{1,0},{2,1},{3,2},{4,3},{5,4},{6,5},{7,6},{9,8},{10,9},{11,10},{12... | collective-permute-start | bytes 4640 | tf_op jit(solution)/shard_map/ppermute | solution.py:21
  (5 other events, 7.5 us)
where the time goes:
time: 264 us; the launch traced here: 259 us
  starting transfers between devices  97.8 us (37%)
  other arithmetic  75.4 us (29%)
  waiting for transfers between devices  45.9 us (17%)
  local copies, waits for them, and re-layouts  38.2 us (14%)
    ppermute x19, starting transfers between devices, with_halo(): lax.ppermute(tail, axis, [(i, (i + 1) % count) for i in range(ends)])  57.1 us
    ppermute x19, waiting for transfers between devices, with_halo(): lax.ppermute(head, axis, [((i + 1) % count, i) for i in range(ends)])  43.4 us
    ppermute x19, starting transfers between devices, with_halo(): lax.ppermute(head, axis, [((i + 1) % count, i) for i in range(ends)])  31.9 us
    div x8, other arithmetic, relax(): return (beside + supply + source) / (4.0 + storage + cond)  29 us
    gather x3, local copies, waits for them, and re-layouts, spread(): return jnp.take(window, window_slot)  17.9 us
    scatter-add x2, other arithmetic, body(): jax.ops.segment_sum(leak, window_slot, 3 * reaches).reshape(3, reaches)  15.4 us
    scatter-add x2, other arithmetic, body(): jax.ops.segment_sum(weight * section_seg[:, None], seg_block, blocks)  15.2 us
    ppermute x4, starting transfers between devices, passed_along(): lax.ppermute(array, axis, [(i, (i + by) % length) for i in range(length)])  8.86 us
  transfers between devices with their start and end apart: 42, of which 16 were waited for; matrix products, arithmetic and copies ran while one was open for 19% of the time, Pallas kernels for 0%

commit v1 on v0

v1 whole, which is shorter than its diff:
```python
import functools

import jax
import jax.numpy as jnp
from jax import lax
from jax.experimental import pallas as pl
from jax.experimental.pallas import tpu as pltpu
from jax.sharding import PartitionSpec as P

PICARD = 2
SWEEPS = 4
L = 128
E = 8
F32 = jnp.float32
BF16 = jnp.bfloat16

DIRS = ((-1, 0), (1, 0), (0, -1), (0, 1), (-1, -1), (-1, 1), (1, -1), (1, 1))
COUNTS = (3, 1, 1, 1)
SUM_STEPS = (1, -1, 2, -2)


def split(x):
    hi = x.astype(BF16)
    return hi, (x - hi.astype(F32)).astype(BF16)


def kernel(
    n_row,
    n_col,
    nets,
    head_in,
    rech,
    stor,
    blk,
    mask,
    conduct,
    reach,
    bed,
    sec0,
    net,
    inflow,
    out_head,
    out_sec,
    place,
    pick,
    put,
    weight,
    slots,
    secseg,
    heads2,
    vals2,
    ga,
    gb,
    supply,
    rhs,
    inv,
    st_send,
    st_recv,
    su_send,
    su_recv,
    *rest,
):
    halo = [rest[6 * e : 6 * e + 6] for e in range(len(COUNTS))]
    st_s, st_r, su_s, su_r, ha_s, ha_r = rest[6 * len(COUNTS) :]
    rows, cols = head_in.shape
    tiles = cols // L
    shift = tiles.bit_length() - 1
    segs = mask.shape[0]
    chunks = segs // L
    h = bed.shape[0]
    reaches = h * L
    ri = lax.axis_index("row")
    ci = lax.axis_index("col")

    def other(dr, dc):
        return (lax.rem(ri + (dr + n_row), n_row), lax.rem(ci + (dc + n_col), n_col))

    partners = list(DIRS) + [(0, 2), (0, -2)]
    barrier = pltpu.get_barrier_semaphore()
    for dr, dc in partners:
        pl.semaphore_signal(
            barrier, inc=1, device_id=other(dr, dc), device_id_type=pl.DeviceIdType.MESH
        )

    def remote(src, dst, send, recv, to):
        return pltpu.make_async_remote_copy(
            src_ref=src,
            dst_ref=dst,
            send_sem=send,
            recv_sem=recv,
            device_id=to,
            device_id_type=pl.DeviceIdType.MESH,
        )

    started = []

    lane = lax.broadcasted_iota(jnp.int32, (L, L), 1)
    sub = lax.broadcasted_iota(jnp.int32, (L, L), 0)
    sub8 = lax.broadcasted_iota(jnp.int32, (8, L), 0)

    net_own = net[...]
    flow = jnp.zeros(net_own.shape, F32)
    for n in range(nets):
        flow = jnp.where(net_own == n, inflow[n], flow)
    st_send[...] = jnp.zeros_like(st_send)
    st_send[0, 0:h] = bed[...]
    st_send[1, 0:h] = flow
    st_send[2, 0:h] = sec0[...]

    b = blk[...]
    place[...] = ((b & (tiles - 1)) * rows + (b >> shift)).astype(F32)

    pl.semaphore_wait(barrier, len(partners))
    st_copies = []
    for k, step in enumerate((1, -1)):
        c = remote(st_send, st_recv.at[k], st_s.at[k], st_r.at[k], other(0, step))
        c.start()
        st_copies.append(c)
    started += st_copies

    own_base = (ri * n_col + ci) * reaches

    def prep(j, _):
        r = pl.ds(pl.multiple_of(j * L, L), L)
        w = mask[r, :].astype(F32) * conduct[r, :]
        weight[r, :] = w
        hi, lo = split(w)
        vals2[r, 0:L] = hi
        vals2[r, L : 2 * L] = lo
        u = reach[pl.ds(j, 1), :] - own_base + reaches
        u = jnp.where(u < 0, u + n_col * reaches, u)
        u = jnp.where(u >= n_col * reaches, u - n_col * reaches, u)
        slots[r, :] = jnp.broadcast_to(u.astype(F32), (L, L)).T.astype(jnp.int32)
        return 0

    lax.fori_loop(0, chunks, prep, 0)

    def build_put(q, _):
        base = q * L
        r = pl.ds(pl.multiple_of(base, L), L)
        for j in range(chunks):
            p = place[j : j + 1, :].astype(jnp.int32) - base
            put[r, j * L : (j + 1) * L] = jnp.where(sub == p, 1.0, 0.0).astype(BF16)
        return 0

    lax.fori_loop(0, rows * tiles // L, build_put, 0)

    def scattered(t):
        r = pl.ds(pl.multiple_of(t * rows, L), rows)
        both = jnp.dot(put[r, :], vals2[...], preferred_element_type=F32)
        return both[:, 0:L] + both[:, L : 2 * L]

    inner = slice(E, E + rows)

    def start_grid(t, _):
        c = pl.ds(pl.multiple_of(t * L, L), L)
        cond = scattered(t)
        s = stor[:, c]
        hd = head_in[:, c]
        ga[inner, c] = hd
        supply[inner, c] = s * hd + rech[:, c]
        inv[inner, c] = 1.0 / (4.0 + s + cond)
        return 0

    lax.fori_loop(0, tiles, start_grid, 0)

    def send_halo(e, arrays):
        s_row, s_col, s_dia, r_row, r_col, r_dia = halo[e]
        for a, x in enumerate(arrays):
            top = x[E : 2 * E, 0:cols]
            bot = x[rows : rows + E, 0:cols]
            s_row[0, a] = top
            s_row[1, a] = bot
            s_col[0, a] = x[inner, 0:L].T[0:E, :]
            s_col[1, a] = x[inner, cols - L : cols].T[L - E : L, :]
            s_dia[0, a] = top[:, 0:L]
            s_dia[1, a] = top[:, cols - L : cols]
            s_dia[2, a] = bot[:, 0:L]
            s_dia[3, a] = bot[:, cols - L : cols]
        copies = []
        for d, (dr, dc) in enumerate(DIRS):
            if dc == 0:
                src, dst = s_row.at[d], r_row.at[d]
            elif dr == 0:
                src, dst = s_col.at[d - 2], r_col.at[d - 2]
            else:
                src, dst = s_dia.at[d - 4], r_dia.at[d - 4]
            c = remote(src, dst, ha_s.at[e, d], ha_r.at[e, d], other(dr, dc))
            c.start()
            copies.append(c)
        return copies

    above = ri > 0
    below = ri < n_row - 1
    lefts = ci > 0
    rights = ci < n_col - 1

    def keep(flag, x):
        return x * jnp.where(flag, 1.0, 0.0).astype(F32)

    def take_halo(e, arrays):
        _, _, _, r_row, r_col, r_dia = halo[e]
        lane8 = lax.broadcasted_iota(jnp.int32, (E, L), 1)
        for a, x in enumerate(arrays):
            x[E + rows : 2 * E + rows, 0:cols] = keep(below, r_row[0, a])
            x[0:E, 0:cols] = keep(above, r_row[1, a])
            beside = jnp.concatenate(
                [
                    keep(rights, r_col[0, a]),
                    jnp.zeros((L - 2 * E, rows), F32),
                    keep(lefts, r_col[1, a]),
                ],
                axis=0,
            )
            x[inner, cols : cols + L] = beside.T
            low = jnp.where(lane8 < L // 2, keep(rights, r_dia[0, a]), keep(lefts, r_dia[1, a]))
            high = jnp.where(lane8 < L // 2, keep(rights, r_dia[2, a]), keep(lefts, r_dia[3, a]))
            x[E + rows : 2 * E + rows, cols : cols + L] = keep(below, low)
            x[0:E, cols : cols + L] = keep(above, high)

    waiting = send_halo(0, (ga, supply, inv))
    started += waiting

    def build_pick(j, _):
        r = pl.ds(pl.multiple_of(j * L, L), L)
        p = jnp.broadcast_to(place[pl.ds(j, 1), :], (L, L)).T.astype(jnp.int32)
        for q in range(rows * tiles // L):
            pick[r, q * L : (q + 1) * L] = jnp.where(p == lane + q * L, 1.0, 0.0).astype(BF16)
        return 0

    lax.fori_loop(0, chunks, build_pick, 0)

    for c in st_copies:
        c.wait_recv()

    def window(k):
        pad = jnp.zeros((8 - 3 * h, L), F32)
        return jnp.concatenate(
            [st_recv[0, k, 0:h], st_send[k, 0:h], st_recv[1, k, 0:h], pad], axis=0
        )

    bed_w = window(0)
    flow_w = window(1)
    sec_w = window(2)

    def spread(sec, fill):
        def one(j, _):
            r = pl.ds(pl.multiple_of(j * L, L), L)
            slot = slots[r, :]
            got = jnp.zeros((L, L), F32)
            for k in range(3 * h):
                got = jnp.where(slot == lane + k * L, sec[k : k + 1, :], got)
            per = jnp.broadcast_to(jnp.sum(got, axis=1, keepdims=True), (L, L))
            secseg[r, :] = per
            if fill:
                hi, lo = split(weight[r, :] * per)
                vals2[r, 0:L] = hi
                vals2[r, L : 2 * L] = lo
            return 0

        lax.fori_loop(0, chunks, one, 0)

    spread(sec_w, False)

    wide = 2 * L if segs % (2 * L) == 0 else L
    groups = (2 * E + rows) // 8

    def sweep(src, dst, last):
        def one(i, carry):
            prev, cur = carry
            r = pl.ds(pl.multiple_of(i * 8, 8), 8)
            nxt = src[pl.ds(pl.multiple_of(jnp.minimum(i + 1, groups - 1) * 8, 8), 8), :]
            s = lax.broadcasted_iota(jnp.int32, cur.shape, 0)
            up = pltpu.roll(jnp.where(s == 7, prev, cur), 1, 0)
            down = pltpu.roll(jnp.where(s == 0, nxt, cur), 7, 0)
            left = pltpu.roll(cur, 1, 1)
            right = pltpu.roll(cur, cols + L - 1, 1)
            new = (((up + down) + (left + right)) + rhs[r, :]) * inv[r, :]
            if last:
                out_head[pl.ds(pl.multiple_of(i * 8 - E, 8), 8), :] = new[:, 0:cols]
            else:
                dst[r, :] = new
            return cur, nxt

        if last:
            lax.fori_loop(1, groups - 1, one, (src[0:8, :], src[8:16, :]))
        else:
            lax.fori_loop(0, groups, one, (src[0:8, :], src[0:8, :]))

    for step in range(PICARD):

        def fill_heads(t, _):
            c = pl.ds(pl.multiple_of(t * L, L), L)
            r = pl.ds(pl.multiple_of(t * rows, L), rows)
            hi, lo = split(ga[inner, c])
            heads2[r, 0:L] = hi
            heads2[r, L : 2 * L] = lo
            return 0

        lax.fori_loop(0, tiles, fill_heads, 0)

        def leaks(j, sums):
            r = pl.ds(pl.multiple_of(j * wide, L), wide)
            both = jnp.dot(pick[r, :], heads2[...], preferred_element_type=F32)
            got = both[:, 0:L] + both[:, L : 2 * L]
            leak = jnp.sum(weight[r, :] * (secseg[r, :] - got), axis=1, keepdims=True)
            slot = slots[r, :]
            lanes = lax.broadcasted_iota(jnp.int32, (wide, L), 1)
            return tuple(
                old + jnp.sum(
                    jnp.where(slot == lanes + k * L, leak, 0.0).reshape(wide // 8, 8, L), axis=0
                )
                for k, old in enumerate(sums)
            )

        sums = lax.fori_loop(
            0, segs // wide, leaks, tuple(jnp.zeros((8, L), F32) for _ in range(3 * h))
        )
        own = jnp.concatenate(
            [jnp.sum(x, axis=0, keepdims=True) for x in sums] + [jnp.zeros((8 - 3 * h, L), F32)],
            axis=0,
        )
        su_send[step] = own
        su_copies = []
        for k, by in enumerate(SUM_STEPS):
            c = remote(
                su_send.at[step],
                su_recv.at[step, k],
                su_s.at[step, k],
                su_r.at[step, k],
                other(0, by),
            )
            c.start()
            su_copies.append(c)
        started += su_copies
        for c in su_copies:
            c.wait_recv()
        zero = jnp.zeros((h, L), F32)
        pad = jnp.zeros((8 - 3 * h, L), F32)
        from_l, from_r, from_ll, from_rr = (su_recv.at[step, k] for k in range(4))
        total = own + jnp.concatenate(
            [
                from_l[h : 2 * h] + from_ll[2 * h : 3 * h],
                from_l[2 * h : 3 * h] + from_r[0:h],
                from_r[h : 2 * h] + from_rr[0:h],
                pad,
            ],
            axis=0,
        )
        x = flow_w - total
        soft = jnp.maximum(x, 0.0) + jnp.log1p(jnp.exp(-jnp.abs(x)))
        sec_w = bed_w + jnp.sqrt(1.0 + soft) - 1.0
        spread(sec_w, True)

        def sources(t, _):
            c = pl.ds(pl.multiple_of(t * L, L), L)
            rhs[inner, c] = supply[inner, c] + scattered(t)
            return 0

        lax.fori_loop(0, tiles, sources, 0)
        mine = send_halo(1 + 2 * step, (rhs,))
        started += mine
        for c in waiting:
            c.wait_recv()
        if step == 0:
            take_halo(0, (ga, supply, inv))
        else:
            take_halo(2, (ga,))
        for c in mine:
            c.wait_recv()
        take_halo(1 + 2 * step, (rhs,))
        bufs = (ga, gb)
        for k in range(SWEEPS):
            last = step == PICARD - 1 and k == SWEEPS - 1
            sweep(bufs[k % 2], bufs[(k + 1) % 2], last)
        if step < PICARD - 1:
            waiting = send_halo(2, (ga,))
            started += waiting

    out_sec[...] = sec_w[h : 2 * h, :]
    for c in started:
        c.wait_send()


def body(n_row, n_col, head, rech, stor, blk, mask, cond, reach, bed, sec, net, inflow):
    rows, cols = head.shape
    segs = blk.shape[0]
    reaches = bed.shape[0]
    blocks = rows * cols // L
    h = reaches // L
    vmem = pl.BlockSpec(memory_space=pltpu.VMEM)
    grid = pltpu.VMEM((rows + 2 * E, cols + L), F32)
    scratch = [
        pltpu.VMEM((segs // L, L), F32),
        pltpu.VMEM((segs, blocks), BF16),
        pltpu.VMEM((blocks, segs), BF16),
        pltpu.VMEM((segs, L), F32),
        pltpu.VMEM((segs, L), jnp.int32),
        pltpu.VMEM((segs, L), F32),
        pltpu.VMEM((blocks, 2 * L), BF16),
        pltpu.VMEM((segs, 2 * L), BF16),
        grid,
        grid,
        grid,
        grid,
        grid,
        pltpu.VMEM((3, 8, L), F32),
        pltpu.VMEM((2, 3, 8, L), F32),
        pltpu.VMEM((PICARD, 8, L), F32),
        pltpu.VMEM((PICARD, 4, 8, L), F32),
    ]
    for n in COUNTS:
        for _ in range(2):
            scratch += [
                pltpu.VMEM((2, n, E, cols), F32),
                pltpu.VMEM((2, n, E, rows), F32),
                pltpu.VMEM((4, n, E, L), F32),
            ]
    dma = pltpu.SemaphoreType.DMA
    scratch += [
        dma((2,)),
        dma((2,)),
        dma((PICARD, 4)),
        dma((PICARD, 4)),
        dma((len(COUNTS), 8)),
        dma((len(COUNTS), 8)),
    ]
    out_head, out_sec = pl.pallas_call(
        functools.partial(kernel, n_row, n_col, inflow.shape[0]),
        out_shape=(
            jax.ShapeDtypeStruct((rows, cols), F32),
            jax.ShapeDtypeStruct((h, L), F32),
        ),
        in_specs=[vmem] * 10 + [pl.BlockSpec(memory_space=pltpu.SMEM)],
        out_specs=(vmem, vmem),
        scratch_shapes=scratch,
        compiler_params=pltpu.CompilerParams(
            collective_id=0, has_side_effects=True, vmem_limit_bytes=56 * 1024 * 1024
        ),
    )(
        head,
        rech,
        stor,
        blk.reshape(segs // L, L),
        mask,
        cond,
        reach.reshape(segs // L, L),
        bed.reshape(h, L),
        sec.reshape(h, L),
        net.reshape(h, L),
        inflow,
    )
    return out_head, out_sec.reshape(reaches)


def solution(mesh):
    placed = (
        P("row", "col"),
        P("row", "col"),
        P("row", "col"),
        P(("row", "col")),
        P(("row", "col"), None),
        P(("row", "col"), None),
        P(("row", "col")),
        P(("row", "col")),
        P(("row", "col")),
        P(("row", "col")),
        P(),
    )
    return jax.shard_map(
        functools.partial(body, mesh.shape["row"], mesh.shape["col"]),
        mesh=mesh,
        in_specs=placed,
        out_specs=(P("row", "col"), P(("row", "col"))),
        check_vma=False,
    )
```

time: 264 us -> 89.7 us (0.34); the launches traced: 259 us -> 89.5 us
  starting transfers between devices: 97.8 us -> 0 us
  Pallas kernels: 0 us -> 85.6 us
  other arithmetic: 75.4 us -> 0 us
  waiting for transfers between devices: 45.9 us -> 0 us
  local copies, waits for them, and re-layouts: 38.2 us -> 3.3 us
    ppermute x42 -> x0, starting transfers between devices: 97.8 us -> none  [the longest x19 57.1 us: with_halo(): lax.ppermute(tail, axis, [(i, (i + 1) % count) for i in range(ends)])]
    pallas_call x0 -> x1, Pallas kernels: none -> 85.6 us  [body(): pl.pallas_call(functools.partial(kernel, n_row, n_col, inflow.shape[0]),...]
    ppermute x42 -> x0, waiting for transfers between devices: 45.9 us -> none  [the longest x19 43.4 us: with_halo(): lax.ppermute(head, axis, [((i + 1) % count, i) for i in range(ends)])]
    scatter-add x5 -> x0, other arithmetic: 37.9 us -> none  [the longest x2 15.4 us: body(): jax.ops.segment_sum(leak, window_slot, 3 * reaches).reshape(3, reaches)]
    div x8 -> x0, other arithmetic: 29 us -> none  [relax(): return (beside + supply + source) / (4.0 + storage + cond)]
    gather x5 -> x0, local copies, waits for them, and re-layouts: 26.1 us -> none  [the longest x3 17.9 us: spread(): return jnp.take(window, window_slot)]
    reshape x5 -> x0, local copies, waits for them, and re-layouts: 10.7 us -> none  [the longest x2 4.1 us: body(): head_seg = jnp.take(head.reshape(blocks, 128), seg_block, axis=0)]
    reduce_sum x2 -> x0, other arithmetic: 3.59 us -> none  [body(): leak = jnp.sum(weight * (section_seg[:, None] - head_seg), axis=1)]
  transfers between devices with their start and end apart: 42 -> 0, of which waited for: 16 -> 0; matrix products, arithmetic and copies ran while one was open for 19% -> 0% of each run, Pallas kernels for 0% -> 0%
where the time goes in v1:
time: 89.7 us; the launch traced here: 89.5 us
  Pallas kernels  85.6 us (95%)
  local copies, waits for them, and re-layouts  3.3 us (4%)
    pallas_call x1, Pallas kernels, body(): pl.pallas_call(functools.partial(kernel, n_row, n_col, inflow.shape[0]),...  85.6 us
    unnamed x4, local copies, waits for them, and re-layouts  3.3 us

profile of v1, /device:TPU:0, one launch (start us, length us, event | category | flops | bytes accessed | tf_op | source)
XLA Modules:
  0.0 89.5 jit_solution(14234177496714667731)
XLA Ops:
  0.6 85.6 %shard_map.122 = (f32[384,1024]{1,0:T(8,128)}, f32[2,128]{1,0:T(2,128)}) custom-call(f32[384,1024]{1,0:T(8,128)} %head_in.1, f32[384,1024]{1,0:T(8,128)} %rech.1, f32[384,1024]{1,0:T(8,128)} %stor.1, s32[8,128]{1,0:T(8,128)} %bitcast.6, s32[1024,128]{1,0:T(8,128)} %mask.1, f32[1024,128]{1,0:T(8,128)} %conduct.1, s32[8,128]{1,0:T(8,128)} %bitcast.7, ...), custom_call_target="tpu_custom_call" | custom-call | tf_op jit(solution)/shard_map/pallas_call | solution.py:428
  86.2 0.0 copy-start
  86.2 2.7 %copy.15 = f32[384,1024]{1,0:T(8,128)} copy(f32[384,1024]{1,0:T(8,128)} %get-tuple-element.8) | data formatting | bytes 3145728
  89.0 0.0 copy-done
  89.0 0.6 copy.16
Async XLA Ops:
  86.2 2.7 %copy-start = (f32[2,128]{1,0:T(2,128)S(1)}, f32[2,128]{1,0:T(2,128)}, u32[]{:S(2)}) copy-start(f32[2,128]{1,0:T(2,128)} %get-tuple-element.5) | copy-start | bytes 3076

commit v2 on v1

--- a/solution.py
+++ b/solution.py
@@ -15,7 +15,7 @@
 BF16 = jnp.bfloat16
 
 DIRS = ((-1, 0), (1, 0), (0, -1), (0, 1), (-1, -1), (-1, 1), (1, -1), (1, 1))
-COUNTS = (3, 1, 1, 1)
+COUNTS = (2, 1, 1, 1)
 SUM_STEPS = (1, -1, 2, -2)
 
 
@@ -61,7 +61,7 @@
     *rest,
 ):
     halo = [rest[6 * e : 6 * e + 6] for e in range(len(COUNTS))]
-    st_s, st_r, su_s, su_r, ha_s, ha_r = rest[6 * len(COUNTS) :]
+    st_s, st_r, su_s, su_r, ha_s, ha_r, lo_s = rest[6 * len(COUNTS) :]
     rows, cols = head_in.shape
     tiles = cols // L
     shift = tiles.bit_length() - 1
@@ -93,6 +93,13 @@
         )
 
     started = []
+    inner = slice(E, E + rows)
+    locals_ = [
+        pltpu.make_async_copy(x, y.at[inner, 0:cols], lo_s.at[k])
+        for k, (x, y) in enumerate(((head_in, ga), (stor, inv), (rech, supply)))
+    ]
+    for c in locals_:
+        c.start()
 
     lane = lax.broadcasted_iota(jnp.int32, (L, L), 1)
     sub = lax.broadcasted_iota(jnp.int32, (L, L), 0)
@@ -143,26 +150,19 @@
             put[r, j * L : (j + 1) * L] = jnp.where(sub == p, 1.0, 0.0).astype(BF16)
         return 0
 
-    lax.fori_loop(0, rows * tiles // L, build_put, 0)
 
     def scattered(t):
         r = pl.ds(pl.multiple_of(t * rows, L), rows)
         both = jnp.dot(put[r, :], vals2[...], preferred_element_type=F32)
         return both[:, 0:L] + both[:, L : 2 * L]
 
-    inner = slice(E, E + rows)
-
     def start_grid(t, _):
         c = pl.ds(pl.multiple_of(t * L, L), L)
         cond = scattered(t)
-        s = stor[:, c]
-        hd = head_in[:, c]
-        ga[inner, c] = hd
-        supply[inner, c] = s * hd + rech[:, c]
+        s = inv[inner, c]
+        supply[inner, c] = s * ga[inner, c] + supply[inner, c]
         inv[inner, c] = 1.0 / (4.0 + s + cond)
         return 0
-
-    lax.fori_loop(0, tiles, start_grid, 0)
 
     def send_halo(e, arrays):
         s_row, s_col, s_dia, r_row, r_col, r_dia = halo[e]
@@ -218,9 +218,6 @@
             x[E + rows : 2 * E + rows, cols : cols + L] = keep(below, low)
             x[0:E, cols : cols + L] = keep(above, high)
 
-    waiting = send_halo(0, (ga, supply, inv))
-    started += waiting
-
     def build_pick(j, _):
         r = pl.ds(pl.multiple_of(j * L, L), L)
         p = jnp.broadcast_to(place[pl.ds(j, 1), :], (L, L)).T.astype(jnp.int32)
@@ -229,6 +226,17 @@
         return 0
 
     lax.fori_loop(0, chunks, build_pick, 0)
+
+    def fill_heads(t, _):
+        c = pl.ds(pl.multiple_of(t * L, L), L)
+        r = pl.ds(pl.multiple_of(t * rows, L), rows)
+        hi, lo = split(ga[inner, c])
+        heads2[r, 0:L] = hi
+        heads2[r, L : 2 * L] = lo
+        return 0
+
+    locals_[0].wait()
+    lax.fori_loop(0, tiles, fill_heads, 0)
 
     for c in st_copies:
         c.wait_recv()
@@ -262,42 +270,41 @@
 
     spread(sec_w, False)
 
-    wide = 2 * L if segs % (2 * L) == 0 else L
+    wide = 4 * L if segs % (4 * L) == 0 else L
     groups = (2 * E + rows) // 8
 
     def sweep(src, dst, last):
-        def one(i, carry):
+        first = 1 if last else 0
+        count = groups - 2 * first
+        unit = max(u for u in range(1, 7) if count % u == 0)
+
+        def some(g, carry):
             prev, cur = carry
-            r = pl.ds(pl.multiple_of(i * 8, 8), 8)
-            nxt = src[pl.ds(pl.multiple_of(jnp.minimum(i + 1, groups - 1) * 8, 8), 8), :]
-            s = lax.broadcasted_iota(jnp.int32, cur.shape, 0)
-            up = pltpu.roll(jnp.where(s == 7, prev, cur), 1, 0)
-            down = pltpu.roll(jnp.where(s == 0, nxt, cur), 7, 0)
-            left = pltpu.roll(cur, 1, 1)
-            right = pltpu.roll(cur, cols + L - 1, 1)
-            new = (((up + down) + (left + right)) + rhs[r, :]) * inv[r, :]
-            if last:
-                out_head[pl.ds(pl.multiple_of(i * 8 - E, 8), 8), :] = new[:, 0:cols]
-            else:
-                dst[r, :] = new
-            return cur, nxt
-
-        if last:
-            lax.fori_loop(1, groups - 1, one, (src[0:8, :], src[8:16, :]))
-        else:
-            lax.fori_loop(0, groups, one, (src[0:8, :], src[0:8, :]))
+            for u in range(unit):
+                i = first + g * unit + u
+                r = pl.ds(pl.multiple_of(i * 8, 8), 8)
+                nxt = src[pl.ds(pl.multiple_of(jnp.minimum(i + 1, groups - 1) * 8, 8), 8), :]
+                s = lax.broadcasted_iota(jnp.int32, cur.shape, 0)
+                up = pltpu.roll(jnp.where(s == 7, prev, cur), 1, 0)
+                down = pltpu.roll(jnp.where(s == 0, nxt, cur), 7, 0)
+                left = pltpu.roll(cur, 1, 1)
+                right = pltpu.roll(cur, cols + L - 1, 1)
+                new = (((up + down) + (left + right)) + rhs[r, :]) * inv[r, :]
+                if last:
+                    out_head[pl.ds(pl.multiple_of(i * 8 - E, 8), 8), :] = new[:, 0:cols]
+                else:
+                    dst[r, :] = new
+                prev, cur = cur, nxt
+            return prev, cur
+
+        lax.fori_loop(0, count // unit, some, (src[0:8, :], src[8 * first : 8 * first + 8, :]))
+
+    def clear_halo(x):
+        x[0:E, :] = jnp.zeros((E, cols + L), F32)
+        x[E + rows : 2 * E + rows, :] = jnp.zeros((E, cols + L), F32)
+        x[inner, cols : cols + L] = jnp.zeros((rows, L), F32)
 
     for step in range(PICARD):
-
-        def fill_heads(t, _):
-            c = pl.ds(pl.multiple_of(t * L, L), L)
-            r = pl.ds(pl.multiple_of(t * rows, L), rows)
-            hi, lo = split(ga[inner, c])
-            heads2[r, 0:L] = hi
-            heads2[r, L : 2 * L] = lo
-            return 0
-
-        lax.fori_loop(0, tiles, fill_heads, 0)
 
         def leaks(j, sums):
             r = pl.ds(pl.multiple_of(j * wide, L), wide)
@@ -333,9 +340,20 @@
             c.start()
             su_copies.append(c)
         started += su_copies
+        if step == 0:
+            lax.fori_loop(0, rows * tiles // L, build_put, 0)
+            locals_[1].wait()
+            locals_[2].wait()
+            lax.fori_loop(0, tiles, start_grid, 0)
+            waiting = send_halo(0, (ga, inv))
+            started += waiting
+        else:
+            for c in waiting:
+                c.wait_recv()
+            take_halo(2, (ga,))
+        clear_halo(rhs)
         for c in su_copies:
             c.wait_recv()
-        zero = jnp.zeros((h, L), F32)
         pad = jnp.zeros((8 - 3 * h, L), F32)
         from_l, from_r, from_ll, from_rr = (su_recv.at[step, k] for k in range(4))
         total = own + jnp.concatenate(
@@ -360,22 +378,28 @@
         lax.fori_loop(0, tiles, sources, 0)
         mine = send_halo(1 + 2 * step, (rhs,))
         started += mine
-        for c in waiting:
-            c.wait_recv()
         if step == 0:
-            take_halo(0, (ga, supply, inv))
-        else:
-            take_halo(2, (ga,))
-        for c in mine:
-            c.wait_recv()
-        take_halo(1 + 2 * step, (rhs,))
+            for c in waiting:
+                c.wait_recv()
+            take_halo(0, (ga, inv))
         bufs = (ga, gb)
         for k in range(SWEEPS):
             last = step == PICARD - 1 and k == SWEEPS - 1
             sweep(bufs[k % 2], bufs[(k + 1) % 2], last)
+            if k == 0:
+                for c in mine:
+                    c.wait_recv()
+                take_halo(1 + 2 * step, (rhs,))
+                for r, c in (
+                    (slice(0, E), slice(0, cols + L)),
+                    (slice(E + rows, 2 * E + rows), slice(0, cols + L)),
+                    (inner, slice(cols, cols + L)),
+                ):
+                    gb[r, c] = gb[r, c] + rhs[r, c] * inv[r, c]
         if step < PICARD - 1:
             waiting = send_halo(2, (ga,))
             started += waiting
+            lax.fori_loop(0, tiles, fill_heads, 0)
 
     out_sec[...] = sec_w[h : 2 * h, :]
     for c in started:
@@ -424,6 +448,7 @@
         dma((PICARD, 4)),
         dma((len(COUNTS), 8)),
         dma((len(COUNTS), 8)),
+        dma((3,)),
     ]
     out_head, out_sec = pl.pallas_call(
         functools.partial(kernel, n_row, n_col, inflow.shape[0]),
@@ -431,7 +456,7 @@
             jax.ShapeDtypeStruct((rows, cols), F32),
             jax.ShapeDtypeStruct((h, L), F32),
         ),
-        in_specs=[vmem] * 10 + [pl.BlockSpec(memory_space=pltpu.SMEM)],
+        in_specs=[pl.BlockSpec(memory_space=pl.ANY)] * 3 + [vmem] * 7 + [pl.BlockSpec(memory_space=pltpu.SMEM)],
         out_specs=(vmem, vmem),
         scratch_shapes=scratch,
         compiler_params=pltpu.CompilerParams(

time: 89.7 us -> 58.4 us (0.65)
  Pallas kernels: 85.6 us -> 54.3 us
    pallas_call x1, Pallas kernels: 85.6 us -> 54.3 us  [body(): pl.pallas_call(functools.partial(kernel, n_row, n_col, inflow.shape[0]),...]
where the time goes in v2:
time: 58.4 us; the launch traced here: 58.3 us
  Pallas kernels  54.3 us (93%)
  local copies, waits for them, and re-layouts  3.3 us (6%)
  between operations  0.65 us (1%)
    pallas_call x1, Pallas kernels, body(): pl.pallas_call(functools.partial(kernel, n_row, n_col, inflow.shape[0]),...  54.3 us
    unnamed x4, local copies, waits for them, and re-layouts  3.3 us

profile of v2, /device:TPU:0, one launch (start us, length us, event | category | flops | bytes accessed | tf_op | source)
XLA Modules:
  0.0 58.3 jit_solution(3374353561000168791)
XLA Ops:
  0.6 54.3 %shard_map.122 = (f32[384,1024]{1,0:T(8,128)}, f32[2,128]{1,0:T(2,128)}) custom-call(f32[384,1024]{1,0:T(8,128)} %head_in.1, f32[384,1024]{1,0:T(8,128)} %rech.1, f32[384,1024]{1,0:T(8,128)} %stor.1, s32[8,128]{1,0:T(8,128)} %bitcast.6, s32[1024,128]{1,0:T(8,128)} %mask.1, f32[1024,128]{1,0:T(8,128)} %conduct.1, s32[8,128]{1,0:T(8,128)} %bitcast.7, ...), custom_call_target="tpu_custom_call" | custom-call | tf_op jit(solution)/shard_map/pallas_call | solution.py:453
  55.0 0.0 copy-start
  55.0 2.7 %copy.15 = f32[384,1024]{1,0:T(8,128)} copy(f32[384,1024]{1,0:T(8,128)} %get-tuple-element.8) | data formatting | bytes 3145728
  57.7 0.0 copy-done
  57.7 0.6 copy.16
Async XLA Ops:
  55.0 2.7 %copy-start = (f32[2,128]{1,0:T(2,128)S(1)}, f32[2,128]{1,0:T(2,128)}, u32[]{:S(2)}) copy-start(f32[2,128]{1,0:T(2,128)} %get-tuple-element.5) | copy-start | bytes 3076

commit v3 on v2

--- a/solution.py
+++ b/solution.py
@@ -16,7 +16,19 @@
 
 DIRS = ((-1, 0), (1, 0), (0, -1), (0, 1), (-1, -1), (-1, 1), (1, -1), (1, 1))
 COUNTS = (2, 1, 1, 1)
+PARTS = 8
 SUM_STEPS = (1, -1, 2, -2)
+
+
+def several(count, most, one):
+    unit = max(u for u in range(1, most + 1) if count % u == 0)
+
+    def some(g, _):
+        for u in range(unit):
+            one(g * unit + u, 0)
+        return 0
+
+    lax.fori_loop(0, count // unit, some, 0)
 
 
 def split(x):
@@ -140,7 +152,7 @@
         slots[r, :] = jnp.broadcast_to(u.astype(F32), (L, L)).T.astype(jnp.int32)
         return 0
 
-    lax.fori_loop(0, chunks, prep, 0)
+    several(chunks, 4, prep)
 
     def build_put(q, _):
         base = q * L
@@ -225,7 +237,7 @@
             pick[r, q * L : (q + 1) * L] = jnp.where(p == lane + q * L, 1.0, 0.0).astype(BF16)
         return 0
 
-    lax.fori_loop(0, chunks, build_pick, 0)
+    several(chunks, 2, build_pick)
 
     def fill_heads(t, _):
         c = pl.ds(pl.multiple_of(t * L, L), L)
@@ -236,7 +248,7 @@
         return 0
 
     locals_[0].wait()
-    lax.fori_loop(0, tiles, fill_heads, 0)
+    several(tiles, 4, fill_heads)
 
     for c in st_copies:
         c.wait_recv()
@@ -266,7 +278,7 @@
                 vals2[r, L : 2 * L] = lo
             return 0
 
-        lax.fori_loop(0, chunks, one, 0)
+        several(chunks, 8, one)
 
     spread(sec_w, False)
 
@@ -276,7 +288,7 @@
     def sweep(src, dst, last):
         first = 1 if last else 0
         count = groups - 2 * first
-        unit = max(u for u in range(1, 7) if count % u == 0)
+        unit = max(u for u in range(1, 13) if count % u == 0)
 
         def some(g, carry):
             prev, cur = carry
@@ -341,10 +353,10 @@
             su_copies.append(c)
         started += su_copies
         if step == 0:
-            lax.fori_loop(0, rows * tiles // L, build_put, 0)
+            several(rows * tiles // L, 3, build_put)
             locals_[1].wait()
             locals_[2].wait()
-            lax.fori_loop(0, tiles, start_grid, 0)
+            several(tiles, 2, start_grid)
             waiting = send_halo(0, (ga, inv))
             started += waiting
         else:
@@ -375,7 +387,7 @@
             rhs[inner, c] = supply[inner, c] + scattered(t)
             return 0
 
-        lax.fori_loop(0, tiles, sources, 0)
+        several(tiles, 2, sources)
         mine = send_halo(1 + 2 * step, (rhs,))
         started += mine
         if step == 0:
@@ -399,11 +411,23 @@
         if step < PICARD - 1:
             waiting = send_halo(2, (ga,))
             started += waiting
-            lax.fori_loop(0, tiles, fill_heads, 0)
+            several(tiles, 4, fill_heads)
 
     out_sec[...] = sec_w[h : 2 * h, :]
     for c in started:
         c.wait_send()
+
+
+def leave(head, sec, out_head, out_sec, sems):
+    part = head.shape[0] // PARTS
+    copies = [pltpu.make_async_copy(sec, out_sec, sems.at[PARTS])]
+    for k in range(PARTS):
+        r = slice(k * part, (k + 1) * part)
+        copies.append(pltpu.make_async_copy(head.at[r, :], out_head.at[r, :], sems.at[k]))
+    for c in copies:
+        c.start()
+    for c in copies:
+        c.wait()
 
 
 def body(n_row, n_col, head, rech, stor, blk, mask, cond, reach, bed, sec, net, inflow):
@@ -475,6 +499,18 @@
         net.reshape(h, L),
         inflow,
     )
+    anywhere = pl.BlockSpec(memory_space=pl.ANY)
+    out_head, out_sec = pl.pallas_call(
+        leave,
+        out_shape=(
+            jax.ShapeDtypeStruct((rows, cols), F32),
+            jax.ShapeDtypeStruct((h, L), F32),
+        ),
+        in_specs=[anywhere] * 2,
+        out_specs=(anywhere,) * 2,
+        scratch_shapes=[pltpu.SemaphoreType.DMA((PARTS + 1,))],
+        compiler_params=pltpu.CompilerParams(vmem_limit_bytes=60 * 1024 * 1024),
+    )(out_head, out_sec)
     return out_head, out_sec.reshape(reaches)
 
 

time: 58.4 us -> 99.3 us (1.70)
  Pallas kernels: 54.3 us -> 98.5 us
  local copies, waits for them, and re-layouts: 3.3 us -> 0 us
    pallas_call x0 -> x1, Pallas kernels: none -> 48.9 us  [body(): pl.pallas_call(leave, out_shape=(jax.ShapeDtypeStruct((rows, cols), F32),...]
    pallas_call x1, Pallas kernels: 54.3 us -> 49.7 us  [body(): pl.pallas_call(functools.partial(kernel, n_row, n_col, inflow.shape[0]),...]
    unnamed x4 -> x0, local copies, waits for them, and re-layouts: 3.3 us -> none
where the time goes in v3:
time: 99.3 us; the launch traced here: 99.2 us
  Pallas kernels  98.5 us (99%)
    pallas_call x1, Pallas kernels, body(): pl.pallas_call(functools.partial(kernel, n_row, n_col, inflow.shape[0]),...  49.7 us
    pallas_call x1, Pallas kernels, body(): pl.pallas_call(leave, out_shape=(jax.ShapeDtypeStruct((rows, cols), F32),...  48.9 us

profile of v3, /device:TPU:0, one launch (start us, length us, event | category | flops | bytes accessed | tf_op | source)
XLA Modules:
  0.0 99.2 jit_solution(11688579572148843671)
XLA Ops:
  0.6 49.7 %shard_map.122 = (f32[384,1024]{1,0:T(8,128)}, f32[2,128]{1,0:T(2,128)}) custom-call(f32[384,1024]{1,0:T(8,128)} %head_in.1, f32[384,1024]{1,0:T(8,128)} %rech.1, f32[384,1024]{1,0:T(8,128)} %stor.1, s32[8,128]{1,0:T(8,128)} %bitcast.6, s32[1024,128]{1,0:T(8,128)} %mask.1, f32[1024,128]{1,0:T(8,128)} %conduct.1, s32[8,128]{1,0:T(8,128)} %bitcast.7, ...), custom_call_target="tpu_custom_call" | custom-call | tf_op jit(solution)/shard_map/pallas_call | solution.py:477
  50.3 48.9 %shard_map.123 = (f32[384,1024]{1,0:T(8,128)}, f32[2,128]{1,0:T(2,128)}) custom-call(f32[384,1024]{1,0:T(8,128)} %get-tuple-element.6.head, f32[2,128]{1,0:T(2,128)} %get-tuple-element.7.sec), custom_call_target="tpu_custom_call" | custom-call | tf_op jit(solution)/shard_map/pallas_call | solution.py:503

commit v4 on v3

--- a/solution.py
+++ b/solution.py
@@ -418,16 +418,21 @@
         c.wait_send()
 
 
-def leave(head, sec, out_head, out_sec, sems):
+def leave(head, sec, out_head, out_sec, held, held_sec, in_sems, out_sems):
     part = head.shape[0] // PARTS
-    copies = [pltpu.make_async_copy(sec, out_sec, sems.at[PARTS])]
+    spans = [(sec, held_sec, out_sec)]
     for k in range(PARTS):
         r = slice(k * part, (k + 1) * part)
-        copies.append(pltpu.make_async_copy(head.at[r, :], out_head.at[r, :], sems.at[k]))
-    for c in copies:
+        spans.append((head.at[r, :], held.at[r, :], out_head.at[r, :]))
+    ins = [pltpu.make_async_copy(x, y, in_sems.at[k]) for k, (x, y, _) in enumerate(spans)]
+    outs = [pltpu.make_async_copy(y, z, out_sems.at[k]) for k, (_, y, z) in enumerate(spans)]
+    for c in ins:
         c.start()
-    for c in copies:
+    for c, d in zip(ins, outs):
         c.wait()
+        d.start()
+    for d in outs:
+        d.wait()
 
 
 def body(n_row, n_col, head, rech, stor, blk, mask, cond, reach, bed, sec, net, inflow):
@@ -508,7 +513,12 @@
         ),
         in_specs=[anywhere] * 2,
         out_specs=(anywhere,) * 2,
-        scratch_shapes=[pltpu.SemaphoreType.DMA((PARTS + 1,))],
+        scratch_shapes=[
+            pltpu.VMEM((rows, cols), F32),
+            pltpu.VMEM((h, L), F32),
+            dma((PARTS + 1,)),
+            dma((PARTS + 1,)),
+        ],
         compiler_params=pltpu.CompilerParams(vmem_limit_bytes=60 * 1024 * 1024),
     )(out_head, out_sec)
     return out_head, out_sec.reshape(reaches)

time: 99.3 us -> 52.8 us (0.53)
  Pallas kernels: 98.5 us -> 52 us
    pallas_call x1, Pallas kernels: 48.9 us -> 2.31 us  [body(): pl.pallas_call(leave, out_shape=(jax.ShapeDtypeStruct((rows, cols), F32),...]
where the time goes in v4:
time: 52.8 us; the launch traced here: 52.6 us
  Pallas kernels  52 us (98%)
  between operations  0.64 us (1%)
    pallas_call x1, Pallas kernels, body(): pl.pallas_call(functools.partial(kernel, n_row, n_col, inflow.shape[0]),...  49.7 us
    pallas_call x1, Pallas kernels, body(): pl.pallas_call(leave, out_shape=(jax.ShapeDtypeStruct((rows, cols), F32),...  2.31 us

profile of v4, /device:TPU:0, one launch (start us, length us, event | category | flops | bytes accessed | tf_op | source)
XLA Modules:
  0.0 52.6 jit_solution(4746158585516622290)
XLA Ops:
  0.6 49.7 %shard_map.122 = (f32[384,1024]{1,0:T(8,128)}, f32[2,128]{1,0:T(2,128)}) custom-call(f32[384,1024]{1,0:T(8,128)} %head_in.1, f32[384,1024]{1,0:T(8,128)} %rech.1, f32[384,1024]{1,0:T(8,128)} %stor.1, s32[8,128]{1,0:T(8,128)} %bitcast.6, s32[1024,128]{1,0:T(8,128)} %mask.1, f32[1024,128]{1,0:T(8,128)} %conduct.1, s32[8,128]{1,0:T(8,128)} %bitcast.7, ...), custom_call_target="tpu_custom_call" | custom-call | tf_op jit(solution)/shard_map/pallas_call | solution.py:482
  50.3 2.3 %shard_map.123 = (f32[384,1024]{1,0:T(8,128)}, f32[2,128]{1,0:T(2,128)}) custom-call(f32[384,1024]{1,0:T(8,128)} %get-tuple-element.6.head, f32[2,128]{1,0:T(2,128)} %get-tuple-element.7.sec), custom_call_target="tpu_custom_call" | custom-call | tf_op jit(solution)/shard_map/pallas_call | solution.py:508
